TPU v7x, 32 devices: a whole 2x2x4 slice. The times are simulated.
32 devices in a mesh: ctx: 8 (over y, x, core), head: 4 (over z).
Axes of the slice: x: 2, y: 2, z: 4, core: 2. Of those that a mesh axis runs over, the one named last changes fastest.
Arguments:
- queries: bfloat16 [1024, 1024], P(('ctx', 'head')), may hold values from -6 to 6
- keys: bfloat16 [1024, 1024], P(('ctx', 'head')), may hold values from -6 to 6
- values: bfloat16 [1024, 2048], P(('ctx', 'head')), may hold values from -6 to 6
- grad_out: bfloat16 [1024, 2048], P('ctx', 'head'), may hold values from -6 to 6
- log_decay: float32 [4, 1024], P('head', 'ctx'), may hold values from -1 to 0
- doc_lengths: int32 [32], replicated, may hold values from 1 to 256, 1024 in all
Outputs:
- retained: bfloat16 [1024, 2048], P('ctx', 'head')
- query_gradient: bfloat16 [1024, 1024], P('ctx', 'head')
- grad_k: bfloat16 [1024, 1024], P('ctx', 'head')
- value_gradient: bfloat16 [1024, 2048], P('ctx', 'head')
Inputs may be any that keep to these rules, and one draw needn't show every extreme that they name: `doc_lengths`: the 32 lengths sum to 1024; the largest is exactly 256.
All inputs are finite; a program needn't handle non-finite values.
Results may differ from a plain program's by a relative error of at most 0.0056.
Values may be sent and summed in bfloat16 or wider, within the bound.
A program may use at most 64 MiB of HBM per device.

v0:
```python
import jax
import jax.numpy as jnp
from jax import lax
from jax.sharding import PartitionSpec as P

BLOCK = 128


def passed_along(block, axis, distance):
    devices = range(lax.axis_size(axis))
    route = [(i - distance, i) for i in devices if i - distance in devices]
    return lax.ppermute(block, axis, route)


def document_ids(doc_lengths, first_place, span_length):
    starts = jnp.cumsum(doc_lengths, dtype=jnp.int32) - doc_lengths
    places = first_place - 1 + jnp.arange(span_length + 1, dtype=jnp.int32)
    return jnp.sum((starts[None, :] <= places[:, None]).astype(jnp.int32), axis=1) - 1


def decay_tables(log_rates, doc_ids, block_size, score_scaling):
    block_count = log_rates.shape[0] // block_size
    cumulated = jnp.cumsum(log_rates.reshape(block_count, block_size), axis=1)
    before = doc_ids[0 : block_count * block_size : block_size]
    own_ids = doc_ids[1:].reshape(block_count, block_size)
    carried = (own_ids == before[:, None]).astype(jnp.float32)
    last_ids = own_ids[:, block_size - 1]
    tail_mask = (own_ids == last_ids[:, None]).astype(jnp.float32)
    block_decay = jnp.exp(cumulated[:, block_size - 1]) * carried[:, block_size - 1]
    row_index = lax.broadcasted_iota(jnp.int32, (block_size, block_size), 0)
    column_index = lax.broadcasted_iota(jnp.int32, (block_size, block_size), 1)
    inside = (own_ids[:, :, None] == own_ids[:, None, :]) & (row_index >= column_index)[None]
    decay_gaps = cumulated[:, :, None] - cumulated[:, None, :]
    weights = jnp.where(inside, jnp.exp(jnp.where(inside, decay_gaps, 0.0)), 0.0) * score_scaling
    per_head_decay_rate = jnp.exp(cumulated) * carried
    tail_decay = jnp.exp(cumulated[:, block_size - 1 :] - cumulated) * tail_mask
    return (weights, per_head_decay_rate, tail_decay, block_decay)


def chain_combine(earlier, follower):
    return (earlier[0] * follower[0], follower[0] * earlier[1] + follower[1])


def offset_list(shard_total):
    return [1] + [1 << level for level in range((shard_total - 1).bit_length())]


def per_device(queries, keys, values, grad_out, log_decay, doc_lengths):
    query_rows, key_rows, value_rows = (
        lax.all_to_all(queries, "head", split_axis=1, concat_axis=0, tiled=True),
        lax.all_to_all(keys, "head", split_axis=1, concat_axis=0, tiled=True),
        lax.all_to_all(values, "head", split_axis=1, concat_axis=0, tiled=True),
    )
    tok_dev, key_dim = key_rows.shape
    value_dim = value_rows.shape[1]
    block_count = tok_dev // BLOCK
    score_scaling = (key_dim * BLOCK) ** (-0.5)
    shard_total = lax.axis_size("ctx")
    doc_ids = document_ids(doc_lengths, lax.axis_index("ctx") * tok_dev, tok_dev)
    weights, per_head_decay_rate, tail_decay, block_decay = decay_tables(
        log_decay[0], doc_ids, BLOCK, score_scaling
    )
    query_block_list = query_rows.reshape(block_count, BLOCK, key_dim)
    key_blocks = key_rows.reshape(block_count, BLOCK, key_dim)
    value_block_list = value_rows.reshape(block_count, BLOCK, value_dim)
    gradient_block_list = grad_out.reshape(block_count, BLOCK, value_dim)
    zero_state = jnp.zeros((key_dim, value_dim), jnp.float32)
    keyed_blocks = (key_blocks * tail_decay[:, :, None]).astype(jnp.bfloat16)
    updates = jnp.einsum(
        "ncd,nce->nde", keyed_blocks, value_block_list, preferred_element_type=jnp.float32
    )
    local_starts = []
    running = zero_state
    factor = jnp.float32(1.0)
    block_index = 0
    local_starts.append(running)
    carry_gains = factor
    running = block_decay[block_index] * running + updates[block_index]
    factor = factor * block_decay[block_index]
    shard_decay = factor
    current = (shard_decay, running)
    for position, offset in enumerate(offset_list(shard_total)):
        pulled = passed_along((current[0], current[1]), "ctx", offset)
        current = pulled if position == 0 else chain_combine(pulled, current)
    incoming = current[1]
    states = jnp.stack([carry_gains * incoming])
    queried = (query_block_list * (per_head_decay_rate * score_scaling)[:, :, None]).astype(
        jnp.bfloat16
    )
    back_updates = jnp.einsum(
        "ncd,nce->nde", queried, gradient_block_list, preferred_element_type=jnp.float32
    )
    local_ends = [zero_state] * block_count
    back_gains = [jnp.float32(1.0)] * block_count
    running = zero_state
    factor = jnp.float32(1.0)
    for block_index in reversed(range(block_count)):
        local_ends[block_index] = running
        back_gains[block_index] = factor
        running = block_decay[block_index] * running + back_updates[block_index]
        factor = factor * block_decay[block_index]
    current = (shard_decay, running)
    for position, offset in enumerate(offset_list(shard_total)):
        pulled = passed_along((current[0], current[1]), "ctx", -offset)
        current = pulled if position == 0 else chain_combine(pulled, current)
    arriving = current[1]
    ends = jnp.stack([back_gains[0] * arriving])
    lowered_state = states.astype(jnp.bfloat16)
    back_low = ends.astype(jnp.bfloat16)
    scores = jnp.einsum(
        "nid,njd->nij", query_block_list, key_blocks, preferred_element_type=jnp.float32
    )
    attention_weights = (scores * weights).astype(jnp.bfloat16)
    retained = (
        jnp.einsum(
            "xho,xoy->xhy", query_block_list, lowered_state, preferred_element_type=jnp.float32
        )
        * (per_head_decay_rate * score_scaling)[:, :, None]
    )
    retained = retained + jnp.einsum(
        "bcv,bvd->bcd", attention_weights, value_block_list, preferred_element_type=jnp.float32
    )
    score_gradient = jnp.einsum(
        "ysb,ytb->yst", gradient_block_list, value_block_list, preferred_element_type=jnp.float32
    )
    gprobs = (score_gradient * weights).astype(jnp.bfloat16)
    query_gradient = (
        jnp.einsum(
            "srj,sqj->srq", gradient_block_list, lowered_state, preferred_element_type=jnp.float32
        )
        * (per_head_decay_rate * score_scaling)[:, :, None]
    )
    query_gradient = query_gradient + jnp.einsum(
        "nij,njd->nid", gprobs, key_blocks, preferred_element_type=jnp.float32
    )
    grad_k = (
        jnp.einsum("nje,nde->njd", value_block_list, back_low, preferred_element_type=jnp.float32)
        * tail_decay[:, :, None]
    )
    grad_k = grad_k + jnp.einsum(
        "nij,nid->njd", gprobs, query_block_list, preferred_element_type=jnp.float32
    )
    value_gradient = (
        jnp.einsum("njd,nde->nje", key_blocks, back_low, preferred_element_type=jnp.float32)
        * tail_decay[:, :, None]
    )
    value_gradient = value_gradient + jnp.einsum(
        "glu,glx->gux", attention_weights, gradient_block_list, preferred_element_type=jnp.float32
    )
    return (
        retained.reshape(tok_dev, value_dim).astype(jnp.bfloat16),
        query_gradient.reshape(tok_dev, key_dim).astype(jnp.bfloat16),
        grad_k.reshape(tok_dev, key_dim).astype(jnp.bfloat16),
        value_gradient.reshape(tok_dev, value_dim).astype(jnp.bfloat16),
    )


def solution(mesh):
    placed = (
        P(("ctx", "head"), None),
        P(("ctx", "head"), None),
        P(("ctx", "head"), None),
        P("ctx", "head"),
        P("head", "ctx"),
        P(),
    )
    return jax.shard_map(
        per_device,
        mesh=mesh,
        in_specs=placed,
        out_specs=(P("ctx", "head"), P("ctx", "head"), P("ctx", "head"), P("ctx", "head")),
        check_vma=False,
    )
```

profile of v0, /device:TPU:5, one launch (start us, length us, event | category | flops | bytes accessed | tf_op | source)
XLA Modules:
  0.0 123.3 jit_solution(668331957569626302)
XLA Ops:
  0.6 0.0 copy-start
  0.6 1.5 %copy.76 = bf16[4,4,8,256]{3,2,0,1:T(8,128)(2,1)} copy(bf16[4,4,8,256]{3,2,1,0:T(8,128)(2,1)} %bitcast.91) | data formatting | bytes 131072 | tf_op jit(solution)/shard_map/all_to_all | solution.py:50
  2.2 4.7 %all-to-all-start.2 = ((bf16[32,4,256]{2,0,1:T(8,128)(2,1)}), bf16[32,4,256]{2,0,1:T(8,128)(2,1)S(1)}, u32[]{:S(2)}, u32[]{:S(2)}) async-start(bf16[32,4,256]{2,0,1:T(8,128)(2,1)} %bitcast.75), calls=%async_computation.2 | async-start | bytes 131072 | tf_op jit(solution)/shard_map/all_to_all | solution.py:50
  6.9 0.1 copy.53
  7.0 0.1 reduce-window.9
  7.0 0.1 reduce
  7.2 0.1 convert_reduce_fusion
  7.3 0.1 fusion.19
  7.3 0.5 slice.19
  7.9 0.6 slice.22
  8.4 0.1 copy-done.4
  8.5 0.3 reduce_window_sum.20
  8.8 0.6 slice.21
  9.4 2.0 %fusion.18 = (f32[128]{0:T(128)S(1)}, f32[128]{0:T(128)S(1)}) fusion(s32[]{:T(128)} %bitcast.1, f32[1,128]{1,0:T(1,128)S(1)} %reduce_window_sum.20, s32[129]{0:T(256)S(1)} %broadcast_add_fusion, f32[]{:T(128)} %bitcast.8, s32[]{:T(128)} %bitcast.7), kind=kLoop, calls=%fused_computation.45 | loop fusion | flops 768 | bytes 2060 | tf_op jit(solution)/shard_map/mul | solution.py:118
  11.4 0.7 compare_bitcast_fusion
  12.8 0.6 slice.20
  14.1 0.6 copy.77
  14.7 0.0 all-to-all-done.2
  14.7 4.5 %all-to-all-start = ((bf16[32,4,256]{2,0,1:T(8,128)(2,1)}), bf16[32,4,256]{2,0,1:T(8,128)(2,1)S(1)}, u32[]{:S(2)}, u32[]{:S(2)}) async-start(bf16[32,4,256]{2,0,1:T(8,128)(2,1)} %bitcast.76), calls=%async_computation | async-start | bytes 131072 | tf_op jit(solution)/shard_map/all_to_all | solution.py:51
  19.2 0.3 convolution_add_fusion
  19.6 3.4 %collective-permute-start.10 = (f32[256,512]{1,0:T(8,128)S(1)}, f32[256,512]{1,0:T(8,128)S(1)}, u32[]{:S(2)}, u32[]{:S(2)}) collective-permute-start(f32[256,512]{1,0:T(8,128)S(1)} %convolution_add_fusion), channel_id=1, source_target_pairs={{4,0},{8,4},{12,8},{16,12},{20,16},{24,20},{28,24},{5,1},{9,5},{13... | collective-permute-start | bytes 1572872 | tf_op jit(solution)/shard_map/ppermute | solution.py:12
  23.0 0.8 all-to-all-done
  23.8 8.7 %all_to_all.48 = bf16[32,4,512]{2,0,1:T(8,128)(2,1)S(1)} all-to-all(bf16[32,4,512]{2,0,1:T(8,128)(2,1)S(1)} %bitcast.89), channel_id=1, replica_groups=mesh['ctx'=8,'head'=4] {'head'}, dimensions={1} | all-to-all | bytes 262144 | tf_op jit(solution)/shard_map/all_to_all | solution.py:52
  32.5 0.3 convolution_add_fusion.1
  32.9 5.4 %collective-permute-start.3 = (f32[256,512]{1,0:T(8,128)S(1)}, f32[256,512]{1,0:T(8,128)S(1)}, u32[]{:S(2)}, u32[]{:S(2)}) collective-permute-start(f32[256,512]{1,0:T(8,128)S(1)} %convolution_add_fusion.1), channel_id=1, source_target_pairs={{0,4},{4,8},{8,12},{12,16},{16,20},{20,24},{24,28},{1,5},{5,9},{9,... | collective-permute-start | bytes 1572872 | tf_op jit(solution)/shard_map/ppermute | solution.py:12
  38.2 1.9 %collective-permute-start.11 = (f32[256,512]{1,0:T(8,128)S(1)}, f32[256,512]{1,0:T(8,128)S(1)}, u32[]{:S(2)}, u32[]{:S(2)}) collective-permute-start(f32[256,512]{1,0:T(8,128)S(1)} %collective-permute-done.10), channel_id=1, source_target_pairs={{4,0},{8,4},{12,8},{16,12},{20,16},{24,20},{28,24},{5,1},{9,5},{13... | collective-permute-start | bytes 1572872 | tf_op jit(solution)/shard_map/ppermute | solution.py:12
  40.2 4.2 %collective-permute-start.7 = (f32[]{:T(128)}, f32[]{:T(128)}, u32[]{:S(2)}, u32[]{:S(2)}) collective-permute-start(f32[]{:T(128)} %bitcast.3), channel_id=1, source_target_pairs={{4,0},{8,4},{12,8},{16,12},{20,16},{24,20},{28,24},{5,1},{9,5},{13... | collective-permute-start | bytes 20 | tf_op jit(solution)/shard_map/ppermute | solution.py:12
  44.4 6.8 %collective-permute-start = (f32[]{:T(128)}, f32[]{:T(128)}, u32[]{:S(2)}, u32[]{:S(2)}) collective-permute-start(f32[]{:T(128)} %bitcast.3), channel_id=1, source_target_pairs={{0,4},{4,8},{8,12},{12,16},{16,20},{20,24},{24,28},{1,5},{5,9},{9,... | collective-permute-start | bytes 20 | tf_op jit(solution)/shard_map/ppermute | solution.py:12
  51.2 3.9 %collective-permute-start.8 = (f32[]{:T(128)}, f32[]{:T(128)}, u32[]{:S(2)}, u32[]{:S(2)}) collective-permute-start(f32[]{:T(128)} %collective-permute-done.7), channel_id=1, source_target_pairs={{4,0},{8,4},{12,8},{16,12},{20,16},{24,20},{28,24},{5,1},{9,5},{13... | collective-permute-start | bytes 20 | tf_op jit(solution)/shard_map/ppermute | solution.py:12
  55.2 1.9 %collective-permute-start.1 = (f32[]{:T(128)}, f32[]{:T(128)}, u32[]{:S(2)}, u32[]{:S(2)}) collective-permute-start(f32[]{:T(128)} %collective-permute-done), channel_id=1, source_target_pairs={{0,4},{4,8},{8,12},{12,16},{16,20},{20,24},{24,28},{1,5},{5,9},{9,... | collective-permute-start | bytes 20 | tf_op jit(solution)/shard_map/ppermute | solution.py:12
  57.1 0.0 collective-permute-done.8
  58.4 7.3 %collective-permute-start.9 = (f32[]{:T(128)}, f32[]{:T(128)}, u32[]{:S(2)}, u32[]{:S(2)}) collective-permute-start(f32[]{:T(128)} %mul.205), channel_id=1, source_target_pairs={{8,0},{12,4},{16,8},{20,12},{24,16},{28,20},{9,1},{13,5},{17,9},{2... | collective-permute-start | bytes 20 | tf_op jit(solution)/shard_map/ppermute | solution.py:12
  66.8 2.6 %collective-permute-start.2 = (f32[]{:T(128)}, f32[]{:T(128)}, u32[]{:S(2)}, u32[]{:S(2)}) collective-permute-start(f32[]{:T(128)} %mul.180), channel_id=1, source_target_pairs={{0,8},{4,12},{8,16},{12,20},{16,24},{20,28},{1,9},{5,13},{9,17},{1... | collective-permute-start | bytes 20 | tf_op jit(solution)/shard_map/ppermute | solution.py:12
  70.1 2.0 %collective-permute-done.2 = f32[]{:T(128)} collective-permute-done((f32[]{:T(128)}, f32[]{:T(128)}, u32[]{:S(2)}, u32[]{:S(2)}) %collective-permute-start.2) | collective-permute-done | bytes 36 | tf_op jit(solution)/shard_map/ppermute | solution.py:12
  72.7 2.0 %collective-permute-start.4 = (f32[256,512]{1,0:T(8,128)S(1)}, f32[256,512]{1,0:T(8,128)S(1)}, u32[]{:S(2)}, u32[]{:S(2)}) collective-permute-start(f32[256,512]{1,0:T(8,128)S(1)} %collective-permute-done.3), channel_id=1, source_target_pairs={{0,4},{4,8},{8,12},{12,16},{16,20},{20,24},{24,28},{1,5},{5,9},{9,... | collective-permute-start | bytes 1572872 | tf_op jit(solution)/shard_map/ppermute | solution.py:12
  74.7 0.0 collective-permute-done.11
  74.7 0.7 multiply_add_fusion.1
  75.5 3.9 %collective-permute-start.12 = (f32[256,512]{1,0:T(8,128)S(1)}, f32[256,512]{1,0:T(8,128)S(1)}, u32[]{:S(2)}, u32[]{:S(2)}) collective-permute-start(f32[256,512]{1,0:T(8,128)S(1)} %multiply_add_fusion.1), channel_id=1, source_target_pairs={{8,0},{12,4},{16,8},{20,12},{24,16},{28,20},{9,1},{13,5},{17,9},{2... | collective-permute-start | bytes 1572872 | tf_op jit(solution)/shard_map/ppermute | solution.py:12
  79.4 0.2 fusion.10
  79.6 0.2 fusion.11
  79.8 2.7 %collective-permute-done.4 = f32[256,512]{1,0:T(8,128)S(1)} collective-permute-done((f32[256,512]{1,0:T(8,128)S(1)}, f32[256,512]{1,0:T(8,128)S(1)}, u32[]{:S(2)}, u32[]{:S(2)}) %collective-permute-start.4) | collective-permute-done | bytes 524320 | tf_op jit(solution)/shard_map/ppermute | solution.py:12
  82.5 0.7 multiply_add_fusion.3
  83.1 1.9 %collective-permute-start.5 = (f32[256,512]{1,0:T(8,128)S(1)}, f32[256,512]{1,0:T(8,128)S(1)}, u32[]{:S(2)}, u32[]{:S(2)}) collective-permute-start(f32[256,512]{1,0:T(8,128)S(1)} %multiply_add_fusion.3), channel_id=1, source_target_pairs={{0,8},{4,12},{8,16},{12,20},{16,24},{20,28},{1,9},{5,13},{9,17},{1... | collective-permute-start | bytes 1572872 | tf_op jit(solution)/shard_map/ppermute | solution.py:12
  85.1 7.8 %collective-permute-done.12 = f32[256,512]{1,0:T(8,128)S(1)} collective-permute-done((f32[256,512]{1,0:T(8,128)S(1)}, f32[256,512]{1,0:T(8,128)S(1)}, u32[]{:S(2)}, u32[]{:S(2)}) %collective-permute-start.12) | collective-permute-done | bytes 524320 | tf_op jit(solution)/shard_map/ppermute | solution.py:12
  92.9 0.1 multiply_add_fusion
  93.0 4.1 %collective-permute-start.13 = (f32[256,512]{1,0:T(8,128)S(1)}, f32[256,512]{1,0:T(8,128)S(1)}, u32[]{:S(2)}, u32[]{:S(2)}) collective-permute-start(f32[256,512]{1,0:T(8,128)S(1)} %multiply_add_fusion), channel_id=1, source_target_pairs={{16,0},{20,4},{24,8},{28,12},{17,1},{21,5},{25,9},{29,13},{18,2},{... | collective-permute-start | bytes 1572872 | tf_op jit(solution)/shard_map/ppermute | solution.py:12
  97.0 0.2 fusion.21
  97.3 0.2 fusion.20
  97.5 8.4 %collective-permute-done.5 = f32[256,512]{1,0:T(8,128)S(1)} collective-permute-done((f32[256,512]{1,0:T(8,128)S(1)}, f32[256,512]{1,0:T(8,128)S(1)}, u32[]{:S(2)}, u32[]{:S(2)}) %collective-permute-start.5) | collective-permute-done | bytes 524320 | tf_op jit(solution)/shard_map/ppermute | solution.py:12
  105.8 0.1 multiply_add_fusion.2
  105.9 1.3 %collective-permute-start.6 = (f32[256,512]{1,0:T(8,128)S(1)}, f32[256,512]{1,0:T(8,128)S(1)}, u32[]{:S(2)}, u32[]{:S(2)}) collective-permute-start(f32[256,512]{1,0:T(8,128)S(1)} %multiply_add_fusion.2), channel_id=1, source_target_pairs={{0,16},{4,20},{8,24},{12,28},{1,17},{5,21},{9,25},{13,29},{2,18},{... | collective-permute-start | bytes 1572872 | tf_op jit(solution)/shard_map/ppermute | solution.py:12
  107.2 0.1 add_convert_fusion
  107.4 0.3 fusion
  107.6 0.2 fusion.3
  107.9 0.8 copy.64
  108.6 0.2 fusion.9
  108.9 0.7 copy.63
  109.6 11.3 %collective-permute-done.6 = f32[256,512]{1,0:T(8,128)S(1)} collective-permute-done((f32[256,512]{1,0:T(8,128)S(1)}, f32[256,512]{1,0:T(8,128)S(1)}, u32[]{:S(2)}, u32[]{:S(2)}) %collective-permute-start.6) | collective-permute-done | bytes 524320 | tf_op jit(solution)/shard_map/ppermute | solution.py:12
  120.9 0.1 add_convert_fusion.1
  121.0 0.3 fusion.1
  121.3 0.2 fusion.8
  121.5 0.7 copy.62
  122.3 0.2 fusion.2
  122.5 0.8 copy.61
  (19 shorter events, 0.1 us)
Async XLA Ops:
  0.6 18.6 %copy-start = (bf16[128,512]{1,0:T(8,128)(2,1)S(1)}, bf16[128,512]{1,0:T(8,128)(2,1)}, u32[]{:S(2)}) copy-start(bf16[128,512]{1,0:T(8,128)(2,1)} %param.9) | copy-start | bytes 393220
  2.2 4.7 %copy-start.3 = (s32[32]{0:T(128)S(1)}, s32[32]{0:T(128)}, u32[]{:S(2)}) copy-start(s32[32]{0:T(128)} %param.11) | copy-start | bytes 388
  2.2 12.6 %all-to-all-start.2 = ((bf16[32,4,256]{2,0,1:T(8,128)(2,1)}), bf16[32,4,256]{2,0,1:T(8,128)(2,1)S(1)}, u32[]{:S(2)}, u32[]{:S(2)}) async-start(bf16[32,4,256]{2,0,1:T(8,128)(2,1)} %bitcast.75), calls=%async_computation.2 | async-start | bytes 131072 | tf_op jit(solution)/shard_map/all_to_all | solution.py:50
  6.9 7.2 %copy-start.2 = (bf16[32,1024]{1,0:T(8,128)(2,1)S(1)}, bf16[32,1024]{1,0:T(8,128)(2,1)}, u32[]{:S(2)}) copy-start(bf16[32,1024]{1,0:T(8,128)(2,1)} %param.7) | copy-start | bytes 196612
  7.9 0.7 copy-start.4
  14.7 9.1 %all-to-all-start = ((bf16[32,4,256]{2,0,1:T(8,128)(2,1)}), bf16[32,4,256]{2,0,1:T(8,128)(2,1)S(1)}, u32[]{:S(2)}, u32[]{:S(2)}) async-start(bf16[32,4,256]{2,0,1:T(8,128)(2,1)} %bitcast.76), calls=%async_computation | async-start | bytes 131072 | tf_op jit(solution)/shard_map/all_to_all | solution.py:51
  19.2 3.8 %copy-start.1 = (bf16[32,2048]{1,0:T(8,128)(2,1)S(1)}, bf16[32,2048]{1,0:T(8,128)(2,1)}, u32[]{:S(2)}) copy-start(bf16[32,2048]{1,0:T(8,128)(2,1)} %param.8) | copy-start | bytes 393220
  19.6 18.7 %collective-permute-start.10 = (f32[256,512]{1,0:T(8,128)S(1)}, f32[256,512]{1,0:T(8,128)S(1)}, u32[]{:S(2)}, u32[]{:S(2)}) collective-permute-start(f32[256,512]{1,0:T(8,128)S(1)} %convolution_add_fusion), channel_id=1, source_target_pairs={{4,0},{8,4},{12,8},{16,12},{20,16},{24,20},{28,24},{5,1},{9,5},{13... | collective-permute-start | bytes 1572872 | tf_op jit(solution)/shard_map/ppermute | solution.py:12
  32.9 39.9 %collective-permute-start.3 = (f32[256,512]{1,0:T(8,128)S(1)}, f32[256,512]{1,0:T(8,128)S(1)}, u32[]{:S(2)}, u32[]{:S(2)}) collective-permute-start(f32[256,512]{1,0:T(8,128)S(1)} %convolution_add_fusion.1), channel_id=1, source_target_pairs={{0,4},{4,8},{8,12},{12,16},{16,20},{20,24},{24,28},{1,5},{5,9},{9,... | collective-permute-start | bytes 1572872 | tf_op jit(solution)/shard_map/ppermute | solution.py:12
  38.2 36.5 %collective-permute-start.11 = (f32[256,512]{1,0:T(8,128)S(1)}, f32[256,512]{1,0:T(8,128)S(1)}, u32[]{:S(2)}, u32[]{:S(2)}) collective-permute-start(f32[256,512]{1,0:T(8,128)S(1)} %collective-permute-done.10), channel_id=1, source_target_pairs={{4,0},{8,4},{12,8},{16,12},{20,16},{24,20},{28,24},{5,1},{9,5},{13... | collective-permute-start | bytes 1572872 | tf_op jit(solution)/shard_map/ppermute | solution.py:12
  40.2 11.1 %collective-permute-start.7 = (f32[]{:T(128)}, f32[]{:T(128)}, u32[]{:S(2)}, u32[]{:S(2)}) collective-permute-start(f32[]{:T(128)} %bitcast.3), channel_id=1, source_target_pairs={{4,0},{8,4},{12,8},{16,12},{20,16},{24,20},{28,24},{5,1},{9,5},{13... | collective-permute-start | bytes 20 | tf_op jit(solution)/shard_map/ppermute | solution.py:12
  44.4 10.8 %collective-permute-start = (f32[]{:T(128)}, f32[]{:T(128)}, u32[]{:S(2)}, u32[]{:S(2)}) collective-permute-start(f32[]{:T(128)} %bitcast.3), channel_id=1, source_target_pairs={{0,4},{4,8},{8,12},{12,16},{16,20},{20,24},{24,28},{1,5},{5,9},{9,... | collective-permute-start | bytes 20 | tf_op jit(solution)/shard_map/ppermute | solution.py:12
  51.2 5.9 %collective-permute-start.8 = (f32[]{:T(128)}, f32[]{:T(128)}, u32[]{:S(2)}, u32[]{:S(2)}) collective-permute-start(f32[]{:T(128)} %collective-permute-done.7), channel_id=1, source_target_pairs={{4,0},{8,4},{12,8},{16,12},{20,16},{24,20},{28,24},{5,1},{9,5},{13... | collective-permute-start | bytes 20 | tf_op jit(solution)/shard_map/ppermute | solution.py:12
  55.2 10.5 %collective-permute-start.1 = (f32[]{:T(128)}, f32[]{:T(128)}, u32[]{:S(2)}, u32[]{:S(2)}) collective-permute-start(f32[]{:T(128)} %collective-permute-done), channel_id=1, source_target_pairs={{0,4},{4,8},{8,12},{12,16},{16,20},{20,24},{24,28},{1,5},{5,9},{9,... | collective-permute-start | bytes 20 | tf_op jit(solution)/shard_map/ppermute | solution.py:12
  58.4 11.1 %collective-permute-start.9 = (f32[]{:T(128)}, f32[]{:T(128)}, u32[]{:S(2)}, u32[]{:S(2)}) collective-permute-start(f32[]{:T(128)} %mul.205), channel_id=1, source_target_pairs={{8,0},{12,4},{16,8},{20,12},{24,16},{28,20},{9,1},{13,5},{17,9},{2... | collective-permute-start | bytes 20 | tf_op jit(solution)/shard_map/ppermute | solution.py:12
  66.8 5.3 %collective-permute-start.2 = (f32[]{:T(128)}, f32[]{:T(128)}, u32[]{:S(2)}, u32[]{:S(2)}) collective-permute-start(f32[]{:T(128)} %mul.180), channel_id=1, source_target_pairs={{0,8},{4,12},{8,16},{12,20},{16,24},{20,28},{1,9},{5,13},{9,17},{1... | collective-permute-start | bytes 20 | tf_op jit(solution)/shard_map/ppermute | solution.py:12
  72.7 9.7 %collective-permute-start.4 = (f32[256,512]{1,0:T(8,128)S(1)}, f32[256,512]{1,0:T(8,128)S(1)}, u32[]{:S(2)}, u32[]{:S(2)}) collective-permute-start(f32[256,512]{1,0:T(8,128)S(1)} %collective-permute-done.3), channel_id=1, source_target_pairs={{0,4},{4,8},{8,12},{12,16},{16,20},{20,24},{24,28},{1,5},{5,9},{9,... | collective-permute-start | bytes 1572872 | tf_op jit(solution)/shard_map/ppermute | solution.py:12
  75.5 17.4 %collective-permute-start.12 = (f32[256,512]{1,0:T(8,128)S(1)}, f32[256,512]{1,0:T(8,128)S(1)}, u32[]{:S(2)}, u32[]{:S(2)}) collective-permute-start(f32[256,512]{1,0:T(8,128)S(1)} %multiply_add_fusion.1), channel_id=1, source_target_pairs={{8,0},{12,4},{16,8},{20,12},{24,16},{28,20},{9,1},{13,5},{17,9},{2... | collective-permute-start | bytes 1572872 | tf_op jit(solution)/shard_map/ppermute | solution.py:12
  83.1 22.7 %collective-permute-start.5 = (f32[256,512]{1,0:T(8,128)S(1)}, f32[256,512]{1,0:T(8,128)S(1)}, u32[]{:S(2)}, u32[]{:S(2)}) collective-permute-start(f32[256,512]{1,0:T(8,128)S(1)} %multiply_add_fusion.3), channel_id=1, source_target_pairs={{0,8},{4,12},{8,16},{12,20},{16,24},{20,28},{1,9},{5,13},{9,17},{1... | collective-permute-start | bytes 1572872 | tf_op jit(solution)/shard_map/ppermute | solution.py:12
  93.0 14.3 %collective-permute-start.13 = (f32[256,512]{1,0:T(8,128)S(1)}, f32[256,512]{1,0:T(8,128)S(1)}, u32[]{:S(2)}, u32[]{:S(2)}) collective-permute-start(f32[256,512]{1,0:T(8,128)S(1)} %multiply_add_fusion), channel_id=1, source_target_pairs={{16,0},{20,4},{24,8},{28,12},{17,1},{21,5},{25,9},{29,13},{18,2},{... | collective-permute-start | bytes 1572872 | tf_op jit(solution)/shard_map/ppermute | solution.py:12
  105.9 15.0 %collective-permute-start.6 = (f32[256,512]{1,0:T(8,128)S(1)}, f32[256,512]{1,0:T(8,128)S(1)}, u32[]{:S(2)}, u32[]{:S(2)}) collective-permute-start(f32[256,512]{1,0:T(8,128)S(1)} %multiply_add_fusion.2), channel_id=1, source_target_pairs={{0,16},{4,20},{8,24},{12,28},{1,17},{5,21},{9,25},{13,29},{2,18},{... | collective-permute-start | bytes 1572872 | tf_op jit(solution)/shard_map/ppermute | solution.py:12
where the time goes:
time: 125 us; the launch traced here: 123 us
  starting transfers between devices  59.9 us (48%)
  waiting for transfers between devices  33 us (26%)
  blocking collectives  8.69 us (7%)
  local copies, waits for them, and re-layouts  7.7 us (6%)
  between operations  5.98 us (5%)
  other arithmetic  5.09 us (4%)
  matrix products  2.88 us (2%)
    ppermute x14, starting transfers between devices, passed_along(): return lax.ppermute(block, axis, route)  50.7 us
    ppermute x14, waiting for transfers between devices, passed_along(): return lax.ppermute(block, axis, route)  32.2 us
    all_to_all x1, blocking collectives, per_device(): lax.all_to_all(values, 'head', split_axis=1, concat_axis=0, tiled=True)  8.69 us
    all_to_all x1, starting transfers between devices, per_device(): lax.all_to_all(queries, 'head', split_axis=1, concat_axis=0, tiled=True)  4.72 us
    all_to_all x1, starting transfers between devices, per_device(): lax.all_to_all(keys, 'head', split_axis=1, concat_axis=0, tiled=True)  4.53 us
    unnamed x14, local copies, waits for them, and re-layouts  3.13 us
  transfers between devices with their start and end apart: 16, of which 6 were waited for; matrix products, arithmetic and copies ran while one was open for 9% of the time, Pallas kernels for 0%

commit v1 on v0

--- a/solution.py
+++ b/solution.py
@@ -1,6 +1,10 @@
 import jax
 import jax.numpy as jnp
+import functools
+
 from jax import lax
+from jax.experimental import pallas as pl
+from jax.experimental.pallas import tpu as pltpu
 from jax.sharding import PartitionSpec as P
 
 BLOCK = 128
@@ -155,19 +159,319 @@
     )
 
 
+CHUNKS = 4
+MESH = pl.DeviceIdType.MESH
+F32, BF16 = jnp.float32, jnp.bfloat16
+
+
+def dot(left, right, left_dim, right_dim):
+    return lax.dot_general(
+        left, right, (((left_dim,), (right_dim,)), ((), ())), preferred_element_type=F32
+    )
+
+
+def kernel(
+    shards,
+    heads,
+    q_ref, k_ref, v_ref, g_ref, log_ref, len_ref,
+    ret_ref, dq_ref, dk_ref, dv_ref,
+    q_all, k_all, v_all, g_all,
+    u_buf, w_buf,
+    f_first_out, f_first_in, f_state_out, f_state_in,
+    b_first_out, b_first_in, b_state_out, b_state_in,
+    ret_buf, dq_buf, dk_buf, dv_buf,
+    head_send, head_recv, local_sem, out_sem,
+    f_first_send, f_first_recv, f_state_send, f_state_recv,
+    b_first_send, b_first_recv, b_state_send, b_state_recv,
+):
+    c, h = lax.axis_index("ctx"), lax.axis_index("head")
+    rows = q_ref.shape[0]
+    tokens, key_dim = q_all.shape
+    value_dim = v_all.shape[1]
+    scale = (key_dim * BLOCK) ** -0.5
+    even = lax.rem(c, 2) == 0
+    odd = jnp.logical_not(even)
+    has_earlier, has_later = c > 0, c < shards - 1
+
+    def row_span(head):
+        return pl.ds(pl.multiple_of(head * rows, rows), rows)
+
+    def head_copy(number, offset, source_head, target_head, place_head):
+        source, gathered = ((q_ref, q_all), (k_ref, k_all), (v_ref, v_all))[number]
+        width = gathered.shape[1]
+        columns = pl.ds(pl.multiple_of(target_head * width, width), width)
+        return source.at[:, columns], gathered.at[row_span(place_head)]
+
+    locals_ = [pltpu.make_async_copy(g_ref, g_all, local_sem.at[3])]
+    for number in range(3):
+        source, target = head_copy(number, 0, h, h, h)
+        locals_.append(pltpu.make_async_copy(source, target, local_sem.at[number]))
+    for copy in locals_:
+        copy.start()
+    local_g, local_parts = locals_[0], locals_[1:]
+
+    barrier = pltpu.get_barrier_semaphore()
+    for offset in range(1, heads):
+        pl.semaphore_signal(
+            barrier, inc=1, device_id=(c, lax.rem(h + offset, heads)), device_id_type=MESH
+        )
+
+    @pl.when(has_earlier)
+    def _():
+        pl.semaphore_signal(barrier, inc=1, device_id=(c - 1, h), device_id_type=MESH)
+
+    @pl.when(has_later)
+    def _():
+        pl.semaphore_signal(barrier, inc=1, device_id=(c + 1, h), device_id_type=MESH)
+
+    pl.semaphore_wait(
+        barrier, heads - 1 + has_earlier.astype(jnp.int32) + has_later.astype(jnp.int32)
+    )
+
+    def sent(number, offset):
+        peer = lax.rem(h + offset, heads)
+        source, target = head_copy(number, offset, h, peer, h)
+        return pltpu.make_async_remote_copy(
+            src_ref=source, dst_ref=target,
+            send_sem=head_send.at[number, offset - 1], recv_sem=head_recv.at[number, offset - 1],
+            device_id=(c, peer), device_id_type=MESH,
+        )
+
+    def received(number, offset):
+        peer = lax.rem(h + heads - offset, heads)
+        source, target = head_copy(number, offset, peer, h, peer)
+        return pltpu.make_async_remote_copy(
+            src_ref=source, dst_ref=target,
+            send_sem=head_send.at[number, offset - 1], recv_sem=head_recv.at[number, offset - 1],
+            device_id=(c, peer), device_id_type=MESH,
+        )
+
+    for number in range(3):
+        for offset in range(1, heads):
+            sent(number, offset).start()
+
+    def arrived(number):
+        local_parts[number].wait()
+        for offset in range(1, heads):
+            received(number, offset).wait_recv()
+
+    i = lax.broadcasted_iota(jnp.int32, (tokens, tokens), 0)
+    j = lax.broadcasted_iota(jnp.int32, (tokens, tokens), 1)
+    cum_col = jnp.sum(jnp.where(j <= i, log_ref[...], 0.0), axis=1, keepdims=True)
+    cum_row = jnp.sum(jnp.where(i == j, cum_col, 0.0), axis=0, keepdims=True)
+    documents = len_ref.shape[1]
+    d = lax.broadcasted_iota(jnp.int32, (documents, documents), 0)
+    e = lax.broadcasted_iota(jnp.int32, (documents, documents), 1)
+    lengths = len_ref[...].astype(F32)
+    starts = jnp.sum(jnp.where(e < d, lengths, 0.0), axis=1, keepdims=True)
+    first = c * tokens
+    places = (lax.broadcasted_iota(jnp.int32, (documents, tokens), 1) + first).astype(F32)
+    doc_row = jnp.sum(jnp.where(starts <= places, 1.0, 0.0), axis=0, keepdims=True)
+    before_place = (lax.broadcasted_iota(jnp.int32, (documents, 1), 1) + (first - 1)).astype(F32)
+    doc_before = jnp.sum(jnp.where(starts <= before_place, 1.0, 0.0), axis=0, keepdims=True)
+    doc_col = jnp.sum(jnp.where(i == j, doc_row, 0.0), axis=1, keepdims=True)
+    last_lane = lax.broadcasted_iota(jnp.int32, (1, tokens), 1) == tokens - 1
+    doc_last = jnp.sum(jnp.where(last_lane, doc_row, 0.0), axis=1, keepdims=True)
+    cum_last = jnp.sum(jnp.where(last_lane, cum_row, 0.0), axis=1, keepdims=True)
+    inside = (doc_col == doc_row) & (j <= i)
+    weights = jnp.where(inside, jnp.exp(jnp.where(inside, cum_col - cum_row, 0.0)), 0.0) * scale
+    rate = jnp.where(doc_col == doc_before, jnp.exp(cum_col), 0.0) * scale
+    tail = jnp.where(doc_col == doc_last, jnp.exp(cum_last - cum_col), 0.0)
+    decay = jnp.where(doc_last == doc_before, jnp.exp(cum_last), 0.0)
+
+    depth = key_dim // CHUNKS
+
+    def passing(update, first_out, first_in, state_out, state_in,
+                first_send, first_recv, state_send, state_recv, opens, target, has_source, has_target):
+        closes = jnp.logical_not(opens)
+
+        def piece(n):
+            return pl.ds(n * depth, depth)
+
+        def first_copy(n):
+            return pltpu.make_async_remote_copy(
+                src_ref=first_out.at[piece(n)], dst_ref=first_in.at[piece(n)],
+                send_sem=first_send.at[n], recv_sem=first_recv.at[n],
+                device_id=(target, h), device_id_type=MESH,
+            )
+
+        def state_copy(n):
+            return pltpu.make_async_remote_copy(
+                src_ref=state_out.at[piece(n)], dst_ref=state_in.at[piece(n)],
+                send_sem=state_send.at[n], recv_sem=state_recv.at[n],
+                device_id=(target, h), device_id_type=MESH,
+            )
+
+        def begin():
+            @pl.when(opens)
+            def _():
+                for n in range(CHUNKS):
+                    first_out[piece(n), :] = update[piece(n), :].astype(BF16)
+                    first_copy(n).start()
+
+            @pl.when(closes & has_target)
+            def _():
+                for n in range(CHUNKS):
+                    first_copy(n).wait_recv()
+                    state_out[piece(n), :] = (
+                        update[piece(n), :] + decay * first_in[piece(n), :].astype(F32)
+                    ).astype(BF16)
+                    state_copy(n).start()
+
+            @pl.when(closes & jnp.logical_not(has_target))
+            def _():
+                for n in range(CHUNKS):
+                    first_copy(n).wait_recv()
+
+        def relay():
+            @pl.when(opens & jnp.logical_not(has_source))
+            def _():
+                state_in[...] = jnp.zeros_like(state_in)
+                for n in range(CHUNKS):
+                    state_out[piece(n), :] = update[piece(n), :].astype(BF16)
+                    state_copy(n).start()
+
+            @pl.when(opens & has_source)
+            def _():
+                for n in range(CHUNKS):
+                    state_copy(n).wait_recv()
+                    state_out[piece(n), :] = (
+                        update[piece(n), :] + decay * state_in[piece(n), :].astype(F32)
+                    ).astype(BF16)
+                    state_copy(n).start()
+
+            @pl.when(closes)
+            def _():
+                for n in range(CHUNKS):
+                    state_copy(n).wait_recv()
+
+        def finish():
+            @pl.when(opens)
+            def _():
+                for n in range(CHUNKS):
+                    first_copy(n).wait_send()
+
+            @pl.when(has_target)
+            def _():
+                for n in range(CHUNKS):
+                    state_copy(n).wait_send()
+
+        return begin, relay, finish
+
+    f_begin, f_relay, f_finish = passing(
+        u_buf, f_first_out, f_first_in, f_state_out, f_state_in,
+        f_first_send, f_first_recv, f_state_send, f_state_recv,
+        even, c + 1, has_earlier, has_later,
+    )
+    b_begin, b_relay, b_finish = passing(
+        w_buf, b_first_out, b_first_in, b_state_out, b_state_in,
+        b_first_send, b_first_recv, b_state_send, b_state_recv,
+        odd, c - 1, has_later, has_earlier,
+    )
+
+    local_g.wait()
+    arrived(0)
+    g = g_all[...]
+    q = q_all[...]
+    queried = (q.astype(F32) * rate).astype(BF16)
+    w_buf[...] = dot(queried, g, 0, 0)
+    b_begin()
+
+    arrived(1)
+    arrived(2)
+    k, v = k_all[...], v_all[...]
+    keyed = (k.astype(F32) * tail).astype(BF16)
+    u_buf[...] = dot(keyed, v, 0, 0)
+    f_begin()
+
+    probs = (dot(q, k, 1, 1) * weights).astype(BF16)
+    gprobs = (dot(g, v, 1, 1) * weights).astype(BF16)
+    dk_part = dot(gprobs, q, 0, 0)
+    dv_part = dot(probs, g, 0, 0)
+
+    outs = [
+        pltpu.make_async_copy(buf, ref, out_sem.at[n])
+        for n, (buf, ref) in enumerate(
+            ((ret_buf, ret_ref), (dq_buf, dq_ref), (dk_buf, dk_ref), (dv_buf, dv_ref))
+        )
+    ]
+    b_relay()
+    back_low = b_state_in[...]
+    dk_buf[...] = (dot(v, back_low, 1, 1) * tail + dk_part).astype(BF16)
+    outs[2].start()
+    dv_buf[...] = (dot(k, back_low, 1, 0) * tail + dv_part).astype(BF16)
+    outs[3].start()
+
+    ret_part = dot(probs, v, 1, 0)
+    dq_part = dot(gprobs, k, 1, 0)
+    f_relay()
+    state_low = f_state_in[...]
+    ret_buf[...] = (dot(q, state_low, 1, 0) * rate + ret_part).astype(BF16)
+    outs[0].start()
+    dq_buf[...] = (dot(g, state_low, 1, 1) * rate + dq_part).astype(BF16)
+    outs[1].start()
+
+    for number in range(3):
+        for offset in range(1, heads):
+            sent(number, offset).wait_send()
+    b_finish()
+    f_finish()
+    for copy in outs:
+        copy.wait()
+
+
+def paired(queries, keys, values, grad_out, log_decay, doc_lengths):
+    shards, heads = lax.axis_size("ctx"), lax.axis_size("head")
+    tokens = queries.shape[0] * heads
+    key_dim, value_dim = keys.shape[1] // heads, values.shape[1] // heads
+    state = pltpu.VMEM((key_dim, value_dim), BF16)
+    total = pltpu.VMEM((key_dim, value_dim), F32)
+    narrow, wide = pltpu.VMEM((tokens, key_dim), BF16), pltpu.VMEM((tokens, value_dim), BF16)
+    dma = pltpu.SemaphoreType.DMA
+    anywhere, vmem = pl.BlockSpec(memory_space=pl.ANY), pl.BlockSpec(memory_space=pltpu.VMEM)
+    return tuple(pl.pallas_call(
+        functools.partial(kernel, shards, heads),
+        out_shape=[
+            jax.ShapeDtypeStruct((tokens, value_dim), BF16),
+            jax.ShapeDtypeStruct((tokens, key_dim), BF16),
+            jax.ShapeDtypeStruct((tokens, key_dim), BF16),
+            jax.ShapeDtypeStruct((tokens, value_dim), BF16),
+        ],
+        in_specs=[anywhere] * 4 + [vmem] * 2,
+        out_specs=[anywhere] * 4,
+        scratch_shapes=[narrow, narrow, wide, wide, total, total]
+        + [state] * 8
+        + [wide, narrow, narrow, wide]
+        + [dma((3, heads - 1)), dma((3, heads - 1)), dma((4,)), dma((4,))]
+        + [dma((CHUNKS,))] * 8,
+        compiler_params=pltpu.CompilerParams(
+            collective_id=0, has_side_effects=True, vmem_limit_bytes=40 * 1024 * 1024
+        ),
+    )(queries, keys, values, grad_out, log_decay, doc_lengths.reshape(1, -1)))
+
+
 def solution(mesh):
-    placed = (
-        P(("ctx", "head"), None),
-        P(("ctx", "head"), None),
-        P(("ctx", "head"), None),
-        P("ctx", "head"),
-        P("head", "ctx"),
-        P(),
-    )
-    return jax.shard_map(
-        per_device,
-        mesh=mesh,
-        in_specs=placed,
-        out_specs=(P("ctx", "head"), P("ctx", "head"), P("ctx", "head"), P("ctx", "head")),
-        check_vma=False,
-    )
+    shards, heads = mesh.shape["ctx"], mesh.shape["head"]
+
+    def whole(queries, keys, values, grad_out, log_decay, doc_lengths):
+        window = queries.shape[0]
+        tokens = window // shards
+        reach = -(-(window // 4 - 1) // tokens)
+        short = reach <= 2 and shards % 2 == 0 and tokens == BLOCK and (tokens // heads) % 16 == 0
+        placed = (
+            P(("ctx", "head"), None),
+            P(("ctx", "head"), None),
+            P(("ctx", "head"), None),
+            P("ctx", "head"),
+            P("head", "ctx"),
+            P(),
+        )
+        return jax.shard_map(
+            paired if short else per_device,
+            mesh=mesh,
+            in_specs=placed,
+            out_specs=(P("ctx", "head"), P("ctx", "head"), P("ctx", "head"), P("ctx", "head")),
+            check_vma=False,
+        )(queries, keys, values, grad_out, log_decay, doc_lengths)
+
+    return whole

time: 125 us -> 27.6 us (0.22); the launches traced: 123 us -> 27.3 us
  starting transfers between devices: 59.9 us -> 0 us
  waiting for transfers between devices: 33 us -> 0 us
  Pallas kernels: 0 us -> 20 us
  blocking collectives: 8.69 us -> 0 us
  between operations: 5.98 us -> 0.66 us
  other arithmetic: 5.09 us -> 0 us
  matrix products: 2.88 us -> 0 us
    ppermute x14 -> x0, starting transfers between devices: 50.7 us -> none  [passed_along(): return lax.ppermute(block, axis, route)]
    ppermute x14 -> x0, waiting for transfers between devices: 32.2 us -> none  [passed_along(): return lax.ppermute(block, axis, route)]
    pallas_call x0 -> x1, Pallas kernels: none -> 20 us  [paired(): pl.pallas_call(functools.partial(kernel, shards, heads), out_shape=[jax.S...]
    all_to_all x2 -> x0, starting transfers between devices: 9.25 us -> none  [the longest x1 4.72 us: per_device(): lax.all_to_all(queries, 'head', split_axis=1, concat_axis=0, tiled=True)]
    all_to_all x1 -> x0, blocking collectives: 8.69 us -> none  [per_device(): lax.all_to_all(values, 'head', split_axis=1, concat_axis=0, tiled=True)]
    unnamed x14 -> x16, local copies, waits for them, and re-layouts: 3.13 us -> 6.71 us
    dot_general x12 -> x0, matrix products: 2.88 us -> none  [the longest x1 0.32 us: per_device(): jnp.einsum('ncd,nce->nde', keyed_blocks, value_block_list, preferred_elem...]
    slice x5 -> x0, local copies, waits for them, and re-layouts: 2.33 us -> none  [the longest x1 0.58 us: decay_tables(): cumulated[:, block_size - 1]]
  transfers between devices with their start and end apart: 16 -> 0, of which waited for: 6 -> 0; matrix products, arithmetic and copies ran while one was open for 9% -> 0% of each run, Pallas kernels for 0% -> 0%
where the time goes in v1:
time: 27.6 us; the launch traced here: 27.3 us
  Pallas kernels  20 us (72%)
  local copies, waits for them, and re-layouts  6.71 us (24%)
  between operations  0.66 us (2%)
    pallas_call x1, Pallas kernels, paired(): pl.pallas_call(functools.partial(kernel, shards, heads), out_shape=[jax.S...  20 us
    unnamed x16, local copies, waits for them, and re-layouts  6.71 us

profile of v1, /device:TPU:5, one launch (start us, length us, event | category | flops | bytes accessed | tf_op | source)
XLA Modules:
  0.0 27.3 jit_solution(3224959180990296928)
XLA Ops:
  0.6 0.0 copy-start.5
  0.6 0.0 copy-start.4
  0.7 0.6 %copy-done.5 = s32[32]{0:T(128)S(1)} copy-done((s32[32]{0:T(128)S(1)}, s32[32]{0:T(128)}, u32[]{:S(2)}) %copy-start.5) | copy-done | bytes 152
  1.3 0.0 copy-done.4
  1.3 0.0 copy-start
  1.3 0.9 %copy-done = bf16[32,2048]{1,0:T(8,128)(2,1)S(1)} copy-done((bf16[32,2048]{1,0:T(8,128)(2,1)S(1)}, bf16[32,2048]{1,0:T(8,128)(2,1)}, u32[]{:S(2)}) %copy-start) | copy-done | bytes 131096
  2.2 0.0 copy-start.1
  2.2 0.9 %copy-done.1 = bf16[128,512]{1,0:T(8,128)(2,1)S(1)} copy-done((bf16[128,512]{1,0:T(8,128)(2,1)S(1)}, bf16[128,512]{1,0:T(8,128)(2,1)}, u32[]{:S(2)}) %copy-start.1) | copy-done | bytes 131096
  3.1 0.0 copy-start.2
  3.1 0.8 %copy-done.2 = bf16[32,1024]{1,0:T(8,128)(2,1)S(1)} copy-done((bf16[32,1024]{1,0:T(8,128)(2,1)S(1)}, bf16[32,1024]{1,0:T(8,128)(2,1)}, u32[]{:S(2)}) %copy-start.2) | copy-done | bytes 65560
  4.0 0.0 copy-start.3
  4.0 0.8 %copy-done.3 = bf16[32,1024]{1,0:T(8,128)(2,1)S(1)} copy-done((bf16[32,1024]{1,0:T(8,128)(2,1)S(1)}, bf16[32,1024]{1,0:T(8,128)(2,1)}, u32[]{:S(2)}) %copy-start.3) | copy-done | bytes 65560
  4.8 20.0 %shard_map.93 = (bf16[128,512]{1,0:T(8,128)(2,1)S(1)}, bf16[128,256]{1,0:T(8,128)(2,1)S(1)}, bf16[128,256]{1,0:T(8,128)(2,1)S(1)}, bf16[128,512]{1,0:T(8,128)(2,1)S(1)}) custom-call(bf16[32,1024]{1,0:T(8,128)(2,1)S(1)} %copy-done.2, bf16[32,1024]{1,0:T(8,128)(2,1)S(1)} %copy-done.3, bf16[32,2048]{1,0:T(8,128)(2,1)S(1)} %copy-done, ...), custom_call_target="tpu_custom_call" | custom-call | tf_op jit(solution)/shard_map/pallas_call | solution.py:432
  24.8 0.7 %copy.14 = bf16[128,512]{1,0:T(8,128)(2,1)} copy(bf16[128,512]{1,0:T(8,128)(2,1)S(1)} %get-tuple-element.8) | data formatting | bytes 262144
  25.4 0.6 %copy.15 = bf16[128,256]{1,0:T(8,128)(2,1)} copy(bf16[128,256]{1,0:T(8,128)(2,1)S(1)} %get-tuple-element.9) | data formatting | bytes 131072
  26.0 0.6 %copy.16 = bf16[128,256]{1,0:T(8,128)(2,1)} copy(bf16[128,256]{1,0:T(8,128)(2,1)S(1)} %get-tuple-element.10) | data formatting | bytes 131072
  26.7 0.7 %copy.17 = bf16[128,512]{1,0:T(8,128)(2,1)} copy(bf16[128,512]{1,0:T(8,128)(2,1)S(1)} %get-tuple-element.11) | data formatting | bytes 262144
Async XLA Ops:
  0.6 0.7 %copy-start.5 = (s32[32]{0:T(128)S(1)}, s32[32]{0:T(128)}, u32[]{:S(2)}) copy-start(s32[32]{0:T(128)} %param.11) | copy-start | bytes 388
  0.6 0.7 %copy-start.4 = (f32[1,128]{1,0:T(1,128)S(1)}, f32[1,128]{1,0:T(1,128)}, u32[]{:S(2)}) copy-start(f32[1,128]{1,0:T(1,128)} %log_ref.1) | copy-start | bytes 1540
  1.3 0.9 %copy-start = (bf16[32,2048]{1,0:T(8,128)(2,1)S(1)}, bf16[32,2048]{1,0:T(8,128)(2,1)}, u32[]{:S(2)}) copy-start(bf16[32,2048]{1,0:T(8,128)(2,1)} %v_ref.1) | copy-start | bytes 393220
  2.2 0.9 %copy-start.1 = (bf16[128,512]{1,0:T(8,128)(2,1)S(1)}, bf16[128,512]{1,0:T(8,128)(2,1)}, u32[]{:S(2)}) copy-start(bf16[128,512]{1,0:T(8,128)(2,1)} %g_ref.1) | copy-start | bytes 393220
  3.1 0.8 %copy-start.2 = (bf16[32,1024]{1,0:T(8,128)(2,1)S(1)}, bf16[32,1024]{1,0:T(8,128)(2,1)}, u32[]{:S(2)}) copy-start(bf16[32,1024]{1,0:T(8,128)(2,1)} %q_ref.1) | copy-start | bytes 196612
  4.0 0.8 %copy-start.3 = (bf16[32,1024]{1,0:T(8,128)(2,1)S(1)}, bf16[32,1024]{1,0:T(8,128)(2,1)}, u32[]{:S(2)}) copy-start(bf16[32,1024]{1,0:T(8,128)(2,1)} %k_ref.1) | copy-start | bytes 196612

commit v2 on v1

--- a/solution.py
+++ b/solution.py
@@ -173,14 +173,14 @@
 def kernel(
     shards,
     heads,
-    q_ref, k_ref, v_ref, g_ref, log_ref, len_ref,
+    q_ref, k_ref, v_ref, g_ref, log_hbm, len_hbm,
     ret_ref, dq_ref, dk_ref, dv_ref,
-    q_all, k_all, v_all, g_all,
+    q_all, k_all, v_all, g_all, log_ref, len_ref,
     u_buf, w_buf,
     f_first_out, f_first_in, f_state_out, f_state_in,
     b_first_out, b_first_in, b_state_out, b_state_in,
-    ret_buf, dq_buf, dk_buf, dv_buf,
-    head_send, head_recv, local_sem, out_sem,
+    ret_part, dq_part, dk_part, dv_part,
+    head_send, head_recv, local_sem,
     f_first_send, f_first_recv, f_state_send, f_state_recv,
     b_first_send, b_first_recv, b_state_send, b_state_recv,
 ):
@@ -188,27 +188,14 @@
     rows = q_ref.shape[0]
     tokens, key_dim = q_all.shape
     value_dim = v_all.shape[1]
+    width = value_dim // CHUNKS
     scale = (key_dim * BLOCK) ** -0.5
     even = lax.rem(c, 2) == 0
     odd = jnp.logical_not(even)
     has_earlier, has_later = c > 0, c < shards - 1
 
-    def row_span(head):
-        return pl.ds(pl.multiple_of(head * rows, rows), rows)
-
-    def head_copy(number, offset, source_head, target_head, place_head):
-        source, gathered = ((q_ref, q_all), (k_ref, k_all), (v_ref, v_all))[number]
-        width = gathered.shape[1]
-        columns = pl.ds(pl.multiple_of(target_head * width, width), width)
-        return source.at[:, columns], gathered.at[row_span(place_head)]
-
-    locals_ = [pltpu.make_async_copy(g_ref, g_all, local_sem.at[3])]
-    for number in range(3):
-        source, target = head_copy(number, 0, h, h, h)
-        locals_.append(pltpu.make_async_copy(source, target, local_sem.at[number]))
-    for copy in locals_:
-        copy.start()
-    local_g, local_parts = locals_[0], locals_[1:]
+    def columns(n):
+        return slice(n * width, (n + 1) * width)
 
     barrier = pltpu.get_barrier_semaphore()
     for offset in range(1, heads):
@@ -224,37 +211,55 @@
     def _():
         pl.semaphore_signal(barrier, inc=1, device_id=(c + 1, h), device_id_type=MESH)
 
+    def head_copy(number, target_head, place_head):
+        if number < 2:
+            source, gathered = ((q_ref, q_all), (k_ref, k_all))[number]
+            span, place = key_dim, pl.ds(0, key_dim)
+            begin = target_head * key_dim
+        else:
+            source, gathered, span = v_ref, v_all, width
+            place = pl.ds((number - 2) * width, width)
+            begin = target_head * value_dim + (number - 2) * width
+        held = pl.ds(pl.multiple_of(place_head * rows, rows), rows)
+        return source.at[:, pl.ds(pl.multiple_of(begin, span), span)], gathered.at[held, place]
+
+    pieces = 2 + CHUNKS
+    own = [
+        pltpu.make_async_copy(*head_copy(number, h, h), local_sem.at[number])
+        for number in range(pieces)
+    ]
+    small = [
+        pltpu.make_async_copy(log_hbm, log_ref, local_sem.at[pieces]),
+        pltpu.make_async_copy(len_hbm, len_ref, local_sem.at[pieces + 1]),
+    ]
+    own_g = pltpu.make_async_copy(g_ref, g_all, local_sem.at[pieces + 2])
+    for copy in small + own[:1] + [own_g] + own[1:]:
+        copy.start()
+
     pl.semaphore_wait(
         barrier, heads - 1 + has_earlier.astype(jnp.int32) + has_later.astype(jnp.int32)
     )
 
-    def sent(number, offset):
-        peer = lax.rem(h + offset, heads)
-        source, target = head_copy(number, offset, h, peer, h)
+    def exchanged(number, offset, incoming):
+        peer = lax.rem(h + (heads - offset if incoming else offset), heads)
+        source, target = head_copy(number, peer, peer if incoming else h)
         return pltpu.make_async_remote_copy(
             src_ref=source, dst_ref=target,
             send_sem=head_send.at[number, offset - 1], recv_sem=head_recv.at[number, offset - 1],
             device_id=(c, peer), device_id_type=MESH,
         )
 
-    def received(number, offset):
-        peer = lax.rem(h + heads - offset, heads)
-        source, target = head_copy(number, offset, peer, h, peer)
-        return pltpu.make_async_remote_copy(
-            src_ref=source, dst_ref=target,
-            send_sem=head_send.at[number, offset - 1], recv_sem=head_recv.at[number, offset - 1],
-            device_id=(c, peer), device_id_type=MESH,
-        )
-
-    for number in range(3):
+    for number in range(pieces):
         for offset in range(1, heads):
-            sent(number, offset).start()
+            exchanged(number, offset, False).start()
 
     def arrived(number):
-        local_parts[number].wait()
+        own[number].wait()
         for offset in range(1, heads):
-            received(number, offset).wait_recv()
-
+            exchanged(number, offset, True).wait_recv()
+
+    for copy in small:
+        copy.wait()
     i = lax.broadcasted_iota(jnp.int32, (tokens, tokens), 0)
     j = lax.broadcasted_iota(jnp.int32, (tokens, tokens), 1)
     cum_col = jnp.sum(jnp.where(j <= i, log_ref[...], 0.0), axis=1, keepdims=True)
@@ -279,71 +284,57 @@
     tail = jnp.where(doc_col == doc_last, jnp.exp(cum_last - cum_col), 0.0)
     decay = jnp.where(doc_last == doc_before, jnp.exp(cum_last), 0.0)
 
-    depth = key_dim // CHUNKS
-
     def passing(update, first_out, first_in, state_out, state_in,
                 first_send, first_recv, state_send, state_recv, opens, target, has_source, has_target):
         closes = jnp.logical_not(opens)
 
-        def piece(n):
-            return pl.ds(n * depth, depth)
-
         def first_copy(n):
             return pltpu.make_async_remote_copy(
-                src_ref=first_out.at[piece(n)], dst_ref=first_in.at[piece(n)],
+                src_ref=first_out.at[n], dst_ref=first_in.at[n],
                 send_sem=first_send.at[n], recv_sem=first_recv.at[n],
                 device_id=(target, h), device_id_type=MESH,
             )
 
         def state_copy(n):
             return pltpu.make_async_remote_copy(
-                src_ref=state_out.at[piece(n)], dst_ref=state_in.at[piece(n)],
+                src_ref=state_out.at[n], dst_ref=state_in.at[n],
                 send_sem=state_send.at[n], recv_sem=state_recv.at[n],
                 device_id=(target, h), device_id_type=MESH,
             )
 
-        def begin():
+        def open_pair(n):
             @pl.when(opens)
             def _():
+                first_out[n] = update[n].astype(BF16)
+                first_copy(n).start()
+
+        def close_pair():
+            @pl.when(closes)
+            def _():
                 for n in range(CHUNKS):
-                    first_out[piece(n), :] = update[piece(n), :].astype(BF16)
-                    first_copy(n).start()
-
-            @pl.when(closes & has_target)
-            def _():
-                for n in range(CHUNKS):
-                    first_copy(n).wait_recv()
-                    state_out[piece(n), :] = (
-                        update[piece(n), :] + decay * first_in[piece(n), :].astype(F32)
-                    ).astype(BF16)
-                    state_copy(n).start()
-
-            @pl.when(closes & jnp.logical_not(has_target))
-            def _():
-                for n in range(CHUNKS):
-                    first_copy(n).wait_recv()
-
-        def relay():
-            @pl.when(opens & jnp.logical_not(has_source))
-            def _():
-                state_in[...] = jnp.zeros_like(state_in)
-                for n in range(CHUNKS):
-                    state_out[piece(n), :] = update[piece(n), :].astype(BF16)
-                    state_copy(n).start()
-
-            @pl.when(opens & has_source)
-            def _():
-                for n in range(CHUNKS):
-                    state_copy(n).wait_recv()
-                    state_out[piece(n), :] = (
-                        update[piece(n), :] + decay * state_in[piece(n), :].astype(F32)
-                    ).astype(BF16)
-                    state_copy(n).start()
-
-            @pl.when(closes)
-            def _():
-                for n in range(CHUNKS):
-                    state_copy(n).wait_recv()
+                    close_chunk(n)
+
+        def close_chunk(n):
+            first_copy(n).wait_recv()
+
+            @pl.when(has_target)
+            def _():
+                state_out[n] = (update[n] + decay * first_in[n].astype(F32)).astype(BF16)
+                state_copy(n).start()
+
+        def relay(n):
+            @pl.when(has_source)
+            def _():
+                state_copy(n).wait_recv()
+
+            @pl.when(jnp.logical_not(has_source))
+            def _():
+                state_in[n] = jnp.zeros(state_in.shape[1:], BF16)
+
+            @pl.when(opens)
+            def _():
+                state_out[n] = (update[n] + decay * state_in[n].astype(F32)).astype(BF16)
+                state_copy(n).start()
 
         def finish():
             @pl.when(opens)
@@ -356,67 +347,80 @@
                 for n in range(CHUNKS):
                     state_copy(n).wait_send()
 
-        return begin, relay, finish
-
-    f_begin, f_relay, f_finish = passing(
+        return open_pair, close_pair, close_chunk, relay, finish
+
+    f_open, _, f_close_chunk, f_relay, f_finish = passing(
         u_buf, f_first_out, f_first_in, f_state_out, f_state_in,
         f_first_send, f_first_recv, f_state_send, f_state_recv,
         even, c + 1, has_earlier, has_later,
     )
-    b_begin, b_relay, b_finish = passing(
+    b_open, b_close, _, b_relay, b_finish = passing(
         w_buf, b_first_out, b_first_in, b_state_out, b_state_in,
         b_first_send, b_first_recv, b_state_send, b_state_recv,
         odd, c - 1, has_later, has_earlier,
     )
 
-    local_g.wait()
+    own_g.wait()
     arrived(0)
-    g = g_all[...]
-    q = q_all[...]
-    queried = (q.astype(F32) * rate).astype(BF16)
-    w_buf[...] = dot(queried, g, 0, 0)
-    b_begin()
+    queried = (q_all[...].astype(F32) * rate).astype(BF16)
+    for n in range(CHUNKS):
+        w_buf[n] = dot(queried, g_all[:, columns(n)], 0, 0)
+        b_open(n)
+    b_close()
 
     arrived(1)
-    arrived(2)
-    k, v = k_all[...], v_all[...]
-    keyed = (k.astype(F32) * tail).astype(BF16)
-    u_buf[...] = dot(keyed, v, 0, 0)
-    f_begin()
-
-    probs = (dot(q, k, 1, 1) * weights).astype(BF16)
-    gprobs = (dot(g, v, 1, 1) * weights).astype(BF16)
-    dk_part = dot(gprobs, q, 0, 0)
-    dv_part = dot(probs, g, 0, 0)
-
-    outs = [
-        pltpu.make_async_copy(buf, ref, out_sem.at[n])
-        for n, (buf, ref) in enumerate(
-            ((ret_buf, ret_ref), (dq_buf, dq_ref), (dk_buf, dk_ref), (dv_buf, dv_ref))
-        )
-    ]
-    b_relay()
-    back_low = b_state_in[...]
-    dk_buf[...] = (dot(v, back_low, 1, 1) * tail + dk_part).astype(BF16)
-    outs[2].start()
-    dv_buf[...] = (dot(k, back_low, 1, 0) * tail + dv_part).astype(BF16)
-    outs[3].start()
-
-    ret_part = dot(probs, v, 1, 0)
-    dq_part = dot(gprobs, k, 1, 0)
-    f_relay()
-    state_low = f_state_in[...]
-    ret_buf[...] = (dot(q, state_low, 1, 0) * rate + ret_part).astype(BF16)
-    outs[0].start()
-    dq_buf[...] = (dot(g, state_low, 1, 1) * rate + dq_part).astype(BF16)
-    outs[1].start()
-
-    for number in range(3):
+    keyed = (k_all[...].astype(F32) * tail).astype(BF16)
+    probs = (dot(q_all[...], k_all[...], 1, 1) * weights).astype(BF16)
+    dv_part[...] = dot(probs, g_all[...], 0, 0)
+    for n in range(CHUNKS):
+        arrived(2 + n)
+        u_buf[n] = dot(keyed, v_all[:, columns(n)], 0, 0)
+        f_open(n)
+        if n:
+            pl.when(odd)(functools.partial(f_close_chunk, n - 1))
+    pl.when(odd)(functools.partial(f_close_chunk, CHUNKS - 1))
+
+    gprobs = (dot(g_all[...], v_all[...], 1, 1) * weights).astype(BF16)
+    dk_part[...] = dot(gprobs, q_all[...], 0, 0)
+    dq_part[...] = dot(gprobs, k_all[...], 1, 0)
+    ret_part[...] = dot(probs, v_all[...], 1, 0)
+
+    total = jnp.zeros((tokens, key_dim), F32)
+    for n in range(CHUNKS):
+        b_relay(n)
+        back = b_state_in[n]
+        dv_ref[:, columns(n)] = (
+            dot(k_all[...], back, 1, 0) * tail + dv_part[:, columns(n)]
+        ).astype(BF16)
+        total += dot(v_all[:, columns(n)], back, 1, 1)
+    dk_ref[...] = (total * tail + dk_part[...]).astype(BF16)
+
+    total = jnp.zeros((tokens, key_dim), F32)
+    for n in range(CHUNKS):
+        f_relay(n)
+        state = f_state_in[n]
+        ret_ref[:, columns(n)] = (
+            dot(q_all[...], state, 1, 0) * rate + ret_part[:, columns(n)]
+        ).astype(BF16)
+        total += dot(g_all[:, columns(n)], state, 1, 1)
+    dq_ref[...] = (total * rate + dq_part[...]).astype(BF16)
+
+    for number in range(pieces):
         for offset in range(1, heads):
-            sent(number, offset).wait_send()
+            exchanged(number, offset, False).wait_send()
     b_finish()
     f_finish()
-    for copy in outs:
+
+
+def leave(*refs):
+    count = len(refs) // 2
+    sem = refs[-1]
+    copies = [
+        pltpu.make_async_copy(refs[n], refs[count + n], sem.at[n]) for n in range(count)
+    ]
+    for copy in copies:
+        copy.start()
+    for copy in copies:
         copy.wait()
 
 
@@ -424,30 +428,41 @@
     shards, heads = lax.axis_size("ctx"), lax.axis_size("head")
     tokens = queries.shape[0] * heads
     key_dim, value_dim = keys.shape[1] // heads, values.shape[1] // heads
-    state = pltpu.VMEM((key_dim, value_dim), BF16)
-    total = pltpu.VMEM((key_dim, value_dim), F32)
-    narrow, wide = pltpu.VMEM((tokens, key_dim), BF16), pltpu.VMEM((tokens, value_dim), BF16)
+    state = pltpu.VMEM((CHUNKS, key_dim, value_dim // CHUNKS), BF16)
+    total = pltpu.VMEM((CHUNKS, key_dim, value_dim // CHUNKS), F32)
     dma = pltpu.SemaphoreType.DMA
-    anywhere, vmem = pl.BlockSpec(memory_space=pl.ANY), pl.BlockSpec(memory_space=pltpu.VMEM)
-    return tuple(pl.pallas_call(
+    hbm, vmem = pl.BlockSpec(memory_space=pltpu.HBM), pl.BlockSpec(memory_space=pltpu.VMEM)
+    wides = (value_dim, key_dim, key_dim, value_dim)
+    outs = [jax.ShapeDtypeStruct((tokens, width), BF16) for width in wides]
+    lengths = doc_lengths.reshape(1, -1)
+    results = pl.pallas_call(
         functools.partial(kernel, shards, heads),
-        out_shape=[
-            jax.ShapeDtypeStruct((tokens, value_dim), BF16),
-            jax.ShapeDtypeStruct((tokens, key_dim), BF16),
-            jax.ShapeDtypeStruct((tokens, key_dim), BF16),
-            jax.ShapeDtypeStruct((tokens, value_dim), BF16),
-        ],
-        in_specs=[anywhere] * 4 + [vmem] * 2,
-        out_specs=[anywhere] * 4,
-        scratch_shapes=[narrow, narrow, wide, wide, total, total]
+        out_shape=outs,
+        in_specs=[hbm] * 6,
+        out_specs=[vmem] * 4,
+        scratch_shapes=[
+            pltpu.VMEM((tokens, width), BF16) for width in (key_dim, key_dim, value_dim, value_dim)
+        ]
+        + [pltpu.VMEM(log_decay.shape, F32), pltpu.VMEM(lengths.shape, jnp.int32)]
+        + [total] * 2
         + [state] * 8
-        + [wide, narrow, narrow, wide]
-        + [dma((3, heads - 1)), dma((3, heads - 1)), dma((4,)), dma((4,))]
+        + [pltpu.VMEM((tokens, width), F32) for width in wides]
+        + [dma((2 + CHUNKS, heads - 1)), dma((2 + CHUNKS, heads - 1)), dma((5 + CHUNKS,))]
         + [dma((CHUNKS,))] * 8,
         compiler_params=pltpu.CompilerParams(
             collective_id=0, has_side_effects=True, vmem_limit_bytes=40 * 1024 * 1024
         ),
-    )(queries, keys, values, grad_out, log_decay, doc_lengths.reshape(1, -1)))
+    )(*[
+        pltpu.with_memory_space_constraint(x, pltpu.HBM)
+        for x in (queries, keys, values, grad_out, log_decay, lengths)
+    ])
+    return tuple(pl.pallas_call(
+        leave,
+        out_shape=outs,
+        in_specs=[vmem] * 4,
+        out_specs=[hbm] * 4,
+        scratch_shapes=[dma((4,))],
+    )(*results))
 
 
 def solution(mesh):

time: 27.6 us -> 24.5 us (0.89)
  local copies, waits for them, and re-layouts: 6.71 us -> 2.53 us
  Pallas kernels: 20 us -> 21.2 us
    unnamed x16 -> x8, local copies, waits for them, and re-layouts: 6.71 us -> 2.53 us
    pallas_call x1 -> x2, Pallas kernels: 20 us -> 21.2 us  [the longest x1 19.4 us: paired(): pl.pallas_call(functools.partial(kernel, shards, heads), out_shape=outs,...]
where the time goes in v2:
time: 24.5 us; the launch traced here: 24.3 us
  Pallas kernels  21.2 us (87%)
  local copies, waits for them, and re-layouts  2.53 us (10%)
  between operations  0.65 us (3%)
    pallas_call x1, Pallas kernels, paired(): pl.pallas_call(functools.partial(kernel, shards, heads), out_shape=outs,...  19.4 us
    unnamed x8, local copies, waits for them, and re-layouts  2.53 us
    pallas_call x1, Pallas kernels, paired(): pl.pallas_call(leave, out_shape=outs, in_specs=[vmem] * 4, out_specs=[hbm...  1.81 us

profile of v2, /device:TPU:5, one launch (start us, length us, event | category | flops | bytes accessed | tf_op | source)
XLA Modules:
  0.0 24.3 jit_solution(9708112630015935513)
XLA Ops:
  0.6 19.4 %shard_map.93 = (bf16[128,512]{1,0:T(8,128)(2,1)S(1)}, bf16[128,256]{1,0:T(8,128)(2,1)S(1)}, bf16[128,256]{1,0:T(8,128)(2,1)S(1)}, bf16[128,512]{1,0:T(8,128)(2,1)S(1)}) custom-call(bf16[32,1024]{1,0:T(8,128)(2,1)} %q_ref.1, bf16[32,1024]{1,0:T(8,128)(2,1)} %k_ref.1, bf16[32,2048]{1,0:T(8,128)(2,1)} %v_ref.1, bf16[128,512]{1,0:T(8,128)(2,1)} %g_ref.1, ...), custom_call_target="tpu_custom_call" | custom-call | tf_op jit(solution)/shard_map/pallas_call | solution.py:438
  20.0 0.0 copy-start
  20.0 0.6 %copy-done = bf16[128,512]{1,0:T(8,128)(2,1)} copy-done((bf16[128,512]{1,0:T(8,128)(2,1)}, bf16[128,512]{1,0:T(8,128)(2,1)S(1)}, u32[]{:S(2)}) %copy-start) | copy-done | bytes 131096
  20.6 0.0 copy-start.1
  20.6 0.6 %copy-done.1 = bf16[128,512]{1,0:T(8,128)(2,1)} copy-done((bf16[128,512]{1,0:T(8,128)(2,1)}, bf16[128,512]{1,0:T(8,128)(2,1)S(1)}, u32[]{:S(2)}) %copy-start.1) | copy-done | bytes 131096
  21.3 0.0 copy-start.2
  21.3 0.6 %copy-done.2 = bf16[128,256]{1,0:T(8,128)(2,1)} copy-done((bf16[128,256]{1,0:T(8,128)(2,1)}, bf16[128,256]{1,0:T(8,128)(2,1)S(1)}, u32[]{:S(2)}) %copy-start.2) | copy-done | bytes 65560
  21.9 0.0 copy-start.3
  21.9 0.6 %copy-done.3 = bf16[128,256]{1,0:T(8,128)(2,1)} copy-done((bf16[128,256]{1,0:T(8,128)(2,1)}, bf16[128,256]{1,0:T(8,128)(2,1)S(1)}, u32[]{:S(2)}) %copy-start.3) | copy-done | bytes 65560
  22.5 1.8 %shard_map.94 = (bf16[128,512]{1,0:T(8,128)(2,1)}, bf16[128,256]{1,0:T(8,128)(2,1)}, bf16[128,256]{1,0:T(8,128)(2,1)}, bf16[128,512]{1,0:T(8,128)(2,1)}) custom-call(bf16[128,512]{1,0:T(8,128)(2,1)} %copy-done, bf16[128,256]{1,0:T(8,128)(2,1)} %copy-done.2, bf16[128,256]{1,0:T(8,128)(2,1)} %copy-done.3, bf16[128,512]{1,0:T(8,128)(2,1)} %copy-done.1), custom_call_target="tpu_custom_call" | custom-call | tf_op jit(solution)/shard_map/pallas_call | solution.py:459
Async XLA Ops:
  20.0 0.7 %copy-start = (bf16[128,512]{1,0:T(8,128)(2,1)}, bf16[128,512]{1,0:T(8,128)(2,1)S(1)}, u32[]{:S(2)}) copy-start(bf16[128,512]{1,0:T(8,128)(2,1)S(1)} %get-tuple-element.8.refs_0_) | copy-start | bytes 393220
  20.6 0.6 %copy-start.1 = (bf16[128,512]{1,0:T(8,128)(2,1)}, bf16[128,512]{1,0:T(8,128)(2,1)S(1)}, u32[]{:S(2)}) copy-start(bf16[128,512]{1,0:T(8,128)(2,1)S(1)} %get-tuple-element.11.refs_3_) | copy-start | bytes 393220
  21.3 0.6 %copy-start.2 = (bf16[128,256]{1,0:T(8,128)(2,1)}, bf16[128,256]{1,0:T(8,128)(2,1)S(1)}, u32[]{:S(2)}) copy-start(bf16[128,256]{1,0:T(8,128)(2,1)S(1)} %get-tuple-element.9.refs_1_) | copy-start | bytes 196612
  21.9 0.6 %copy-start.3 = (bf16[128,256]{1,0:T(8,128)(2,1)}, bf16[128,256]{1,0:T(8,128)(2,1)S(1)}, u32[]{:S(2)}) copy-start(bf16[128,256]{1,0:T(8,128)(2,1)S(1)} %get-tuple-element.10.refs_2_) | copy-start | bytes 196612

commit v3 on v2

--- a/solution.py
+++ b/solution.py
@@ -160,6 +160,7 @@
 
 
 CHUNKS = 4
+PARTS = 2
 MESH = pl.DeviceIdType.MESH
 F32, BF16 = jnp.float32, jnp.bfloat16
 
@@ -189,6 +190,7 @@
     tokens, key_dim = q_all.shape
     value_dim = v_all.shape[1]
     width = value_dim // CHUNKS
+    part = value_dim // PARTS
     scale = (key_dim * BLOCK) ** -0.5
     even = lax.rem(c, 2) == 0
     odd = jnp.logical_not(even)
@@ -217,13 +219,13 @@
             span, place = key_dim, pl.ds(0, key_dim)
             begin = target_head * key_dim
         else:
-            source, gathered, span = v_ref, v_all, width
-            place = pl.ds((number - 2) * width, width)
-            begin = target_head * value_dim + (number - 2) * width
+            source, gathered, span = v_ref, v_all, part
+            place = pl.ds((number - 2) * part, part)
+            begin = target_head * value_dim + (number - 2) * part
         held = pl.ds(pl.multiple_of(place_head * rows, rows), rows)
         return source.at[:, pl.ds(pl.multiple_of(begin, span), span)], gathered.at[held, place]
 
-    pieces = 2 + CHUNKS
+    pieces = 2 + PARTS
     own = [
         pltpu.make_async_copy(*head_copy(number, h, h), local_sem.at[number])
         for number in range(pieces)
@@ -249,9 +251,8 @@
             device_id=(c, peer), device_id_type=MESH,
         )
 
-    for number in range(pieces):
-        for offset in range(1, heads):
-            exchanged(number, offset, False).start()
+    for offset in range(1, heads):
+        exchanged(0, offset, False).start()
 
     def arrived(number):
         own[number].wait()
@@ -284,6 +285,10 @@
     tail = jnp.where(doc_col == doc_last, jnp.exp(cum_last - cum_col), 0.0)
     decay = jnp.where(doc_last == doc_before, jnp.exp(cum_last), 0.0)
 
+    for number in range(1, pieces):
+        for offset in range(1, heads):
+            exchanged(number, offset, False).start()
+
     def passing(update, first_out, first_in, state_out, state_in,
                 first_send, first_recv, state_send, state_recv, opens, target, has_source, has_target):
         closes = jnp.logical_not(opens)
@@ -362,19 +367,20 @@
 
     own_g.wait()
     arrived(0)
-    queried = (q_all[...].astype(F32) * rate).astype(BF16)
+    queried = (q_all[...].astype(F32) * rate).T.astype(BF16)
     for n in range(CHUNKS):
-        w_buf[n] = dot(queried, g_all[:, columns(n)], 0, 0)
+        w_buf[n] = dot(queried, g_all[:, columns(n)], 1, 0)
         b_open(n)
     b_close()
 
     arrived(1)
-    keyed = (k_all[...].astype(F32) * tail).astype(BF16)
+    keyed = (k_all[...].astype(F32) * tail).T.astype(BF16)
     probs = (dot(q_all[...], k_all[...], 1, 1) * weights).astype(BF16)
     dv_part[...] = dot(probs, g_all[...], 0, 0)
     for n in range(CHUNKS):
-        arrived(2 + n)
-        u_buf[n] = dot(keyed, v_all[:, columns(n)], 0, 0)
+        if n % (CHUNKS // PARTS) == 0:
+            arrived(2 + n // (CHUNKS // PARTS))
+        u_buf[n] = dot(keyed, v_all[:, columns(n)], 1, 0)
         f_open(n)
         if n:
             pl.when(odd)(functools.partial(f_close_chunk, n - 1))
@@ -437,7 +443,7 @@
     lengths = doc_lengths.reshape(1, -1)
     results = pl.pallas_call(
         functools.partial(kernel, shards, heads),
-        out_shape=outs,
+        out_shape=[pltpu.VMEM((tokens, width), BF16) for width in wides],
         in_specs=[hbm] * 6,
         out_specs=[vmem] * 4,
         scratch_shapes=[
@@ -447,7 +453,7 @@
         + [total] * 2
         + [state] * 8
         + [pltpu.VMEM((tokens, width), F32) for width in wides]
-        + [dma((2 + CHUNKS, heads - 1)), dma((2 + CHUNKS, heads - 1)), dma((5 + CHUNKS,))]
+        + [dma((2 + PARTS, heads - 1)), dma((2 + PARTS, heads - 1)), dma((5 + PARTS,))]
         + [dma((CHUNKS,))] * 8,
         compiler_params=pltpu.CompilerParams(
             collective_id=0, has_side_effects=True, vmem_limit_bytes=40 * 1024 * 1024

time: 24.5 us -> 24.4 us (level)
  no operation moved by 1% of the time
where the time goes in v3:
time: 24.4 us; the launch traced here: 24.3 us
  Pallas kernels  21.1 us (86%)
  local copies, waits for them, and re-layouts  2.53 us (10%)
  between operations  0.65 us (3%)
    pallas_call x1, Pallas kernels, paired(): pl.pallas_call(functools.partial(kernel, shards, heads), out_shape=[pltpu...  19.3 us
    unnamed x8, local copies, waits for them, and re-layouts  2.53 us
    pallas_call x1, Pallas kernels, paired(): pl.pallas_call(leave, out_shape=outs, in_specs=[vmem] * 4, out_specs=[hbm...  1.81 us

profile of v3, /device:TPU:5, one launch (start us, length us, event | category | flops | bytes accessed | tf_op | source)
XLA Modules:
  0.0 24.3 jit_solution(13177073596624502921)
XLA Ops:
  0.6 19.3 %shard_map.93 = (bf16[128,512]{1,0:T(8,128)(2,1)S(1)}, bf16[128,256]{1,0:T(8,128)(2,1)S(1)}, bf16[128,256]{1,0:T(8,128)(2,1)S(1)}, bf16[128,512]{1,0:T(8,128)(2,1)S(1)}) custom-call(bf16[32,1024]{1,0:T(8,128)(2,1)} %q_ref.1, bf16[32,1024]{1,0:T(8,128)(2,1)} %k_ref.1, bf16[32,2048]{1,0:T(8,128)(2,1)} %v_ref.1, bf16[128,512]{1,0:T(8,128)(2,1)} %g_ref.1, ...), custom_call_target="tpu_custom_call" | custom-call | tf_op jit(solution)/shard_map/pallas_call | solution.py:444
  20.0 0.0 copy-start
  20.0 0.6 %copy-done = bf16[128,512]{1,0:T(8,128)(2,1)} copy-done((bf16[128,512]{1,0:T(8,128)(2,1)}, bf16[128,512]{1,0:T(8,128)(2,1)S(1)}, u32[]{:S(2)}) %copy-start) | copy-done | bytes 131096
  20.6 0.0 copy-start.1
  20.6 0.6 %copy-done.1 = bf16[128,512]{1,0:T(8,128)(2,1)} copy-done((bf16[128,512]{1,0:T(8,128)(2,1)}, bf16[128,512]{1,0:T(8,128)(2,1)S(1)}, u32[]{:S(2)}) %copy-start.1) | copy-done | bytes 131096
  21.3 0.0 copy-start.2
  21.3 0.6 %copy-done.2 = bf16[128,256]{1,0:T(8,128)(2,1)} copy-done((bf16[128,256]{1,0:T(8,128)(2,1)}, bf16[128,256]{1,0:T(8,128)(2,1)S(1)}, u32[]{:S(2)}) %copy-start.2) | copy-done | bytes 65560
  21.9 0.0 copy-start.3
  21.9 0.6 %copy-done.3 = bf16[128,256]{1,0:T(8,128)(2,1)} copy-done((bf16[128,256]{1,0:T(8,128)(2,1)}, bf16[128,256]{1,0:T(8,128)(2,1)S(1)}, u32[]{:S(2)}) %copy-start.3) | copy-done | bytes 65560
  22.5 1.8 %shard_map.94 = (bf16[128,512]{1,0:T(8,128)(2,1)}, bf16[128,256]{1,0:T(8,128)(2,1)}, bf16[128,256]{1,0:T(8,128)(2,1)}, bf16[128,512]{1,0:T(8,128)(2,1)}) custom-call(bf16[128,512]{1,0:T(8,128)(2,1)} %copy-done, bf16[128,256]{1,0:T(8,128)(2,1)} %copy-done.2, bf16[128,256]{1,0:T(8,128)(2,1)} %copy-done.3, bf16[128,512]{1,0:T(8,128)(2,1)} %copy-done.1), custom_call_target="tpu_custom_call" | custom-call | tf_op jit(solution)/shard_map/pallas_call | solution.py:465
Async XLA Ops:
  20.0 0.7 %copy-start = (bf16[128,512]{1,0:T(8,128)(2,1)}, bf16[128,512]{1,0:T(8,128)(2,1)S(1)}, u32[]{:S(2)}) copy-start(bf16[128,512]{1,0:T(8,128)(2,1)S(1)} %get-tuple-element.8.refs_0_) | copy-start | bytes 393220
  20.6 0.6 %copy-start.1 = (bf16[128,512]{1,0:T(8,128)(2,1)}, bf16[128,512]{1,0:T(8,128)(2,1)S(1)}, u32[]{:S(2)}) copy-start(bf16[128,512]{1,0:T(8,128)(2,1)S(1)} %get-tuple-element.11.refs_3_) | copy-start | bytes 393220
  21.3 0.6 %copy-start.2 = (bf16[128,256]{1,0:T(8,128)(2,1)}, bf16[128,256]{1,0:T(8,128)(2,1)S(1)}, u32[]{:S(2)}) copy-start(bf16[128,256]{1,0:T(8,128)(2,1)S(1)} %get-tuple-element.9.refs_1_) | copy-start | bytes 196612
  21.9 0.6 %copy-start.3 = (bf16[128,256]{1,0:T(8,128)(2,1)}, bf16[128,256]{1,0:T(8,128)(2,1)S(1)}, u32[]{:S(2)}) copy-start(bf16[128,256]{1,0:T(8,128)(2,1)S(1)} %get-tuple-element.10.refs_2_) | copy-start | bytes 196612

commit v4 on v3

--- a/solution.py
+++ b/solution.py
@@ -285,7 +285,7 @@
     tail = jnp.where(doc_col == doc_last, jnp.exp(cum_last - cum_col), 0.0)
     decay = jnp.where(doc_last == doc_before, jnp.exp(cum_last), 0.0)
 
-    for number in range(1, pieces):
+    for number in range(1, pieces - 1):
         for offset in range(1, heads):
             exchanged(number, offset, False).start()
 
@@ -365,50 +365,67 @@
         odd, c - 1, has_later, has_earlier,
     )
 
+    per_part = CHUNKS // PARTS
+
+    def halves(n):
+        return slice(n * part, (n + 1) * part)
+
     own_g.wait()
     arrived(0)
     queried = (q_all[...].astype(F32) * rate).T.astype(BF16)
-    for n in range(CHUNKS):
-        w_buf[n] = dot(queried, g_all[:, columns(n)], 1, 0)
-        b_open(n)
+    for m in range(PARTS):
+        product = dot(queried, g_all[:, halves(m)], 1, 0)
+        for n in range(per_part):
+            w_buf[m * per_part + n] = product[:, columns(n)]
+            b_open(m * per_part + n)
+    for offset in range(1, heads):
+        exchanged(pieces - 1, offset, False).start()
     b_close()
 
     arrived(1)
     keyed = (k_all[...].astype(F32) * tail).T.astype(BF16)
     probs = (dot(q_all[...], k_all[...], 1, 1) * weights).astype(BF16)
-    dv_part[...] = dot(probs, g_all[...], 0, 0)
-    for n in range(CHUNKS):
-        if n % (CHUNKS // PARTS) == 0:
-            arrived(2 + n // (CHUNKS // PARTS))
-        u_buf[n] = dot(keyed, v_all[:, columns(n)], 1, 0)
-        f_open(n)
-        if n:
-            pl.when(odd)(functools.partial(f_close_chunk, n - 1))
-    pl.when(odd)(functools.partial(f_close_chunk, CHUNKS - 1))
+    for m in range(PARTS):
+        arrived(2 + m)
+        product = dot(keyed, v_all[:, halves(m)], 1, 0)
+        for n in range(per_part):
+            u_buf[m * per_part + n] = product[:, columns(n)]
+            f_open(m * per_part + n)
+        if m == 0:
+            dv_part[...] = dot(probs, g_all[...], 0, 0)
+
+        @pl.when(odd)
+        def _():
+            for n in range(per_part):
+                f_close_chunk(m * per_part + n)
 
     gprobs = (dot(g_all[...], v_all[...], 1, 1) * weights).astype(BF16)
     dk_part[...] = dot(gprobs, q_all[...], 0, 0)
     dq_part[...] = dot(gprobs, k_all[...], 1, 0)
     ret_part[...] = dot(probs, v_all[...], 1, 0)
 
+    def joined(relay, state_in, m):
+        chunks = range(m * per_part, (m + 1) * per_part)
+        for n in chunks:
+            relay(n)
+        return jnp.concatenate([state_in[n] for n in chunks], axis=1)
+
     total = jnp.zeros((tokens, key_dim), F32)
-    for n in range(CHUNKS):
-        b_relay(n)
-        back = b_state_in[n]
-        dv_ref[:, columns(n)] = (
-            dot(k_all[...], back, 1, 0) * tail + dv_part[:, columns(n)]
+    for m in range(PARTS):
+        back = joined(b_relay, b_state_in, m)
+        dv_ref[:, halves(m)] = (
+            dot(k_all[...], back, 1, 0) * tail + dv_part[:, halves(m)]
         ).astype(BF16)
-        total += dot(v_all[:, columns(n)], back, 1, 1)
+        total += dot(v_all[:, halves(m)], back, 1, 1)
     dk_ref[...] = (total * tail + dk_part[...]).astype(BF16)
 
     total = jnp.zeros((tokens, key_dim), F32)
-    for n in range(CHUNKS):
-        f_relay(n)
-        state = f_state_in[n]
-        ret_ref[:, columns(n)] = (
-            dot(q_all[...], state, 1, 0) * rate + ret_part[:, columns(n)]
+    for m in range(PARTS):
+        state = joined(f_relay, f_state_in, m)
+        ret_ref[:, halves(m)] = (
+            dot(q_all[...], state, 1, 0) * rate + ret_part[:, halves(m)]
         ).astype(BF16)
-        total += dot(g_all[:, columns(n)], state, 1, 1)
+        total += dot(g_all[:, halves(m)], state, 1, 1)
     dq_ref[...] = (total * rate + dq_part[...]).astype(BF16)
 
     for number in range(pieces):
@@ -468,6 +485,7 @@
         in_specs=[vmem] * 4,
         out_specs=[hbm] * 4,
         scratch_shapes=[dma((4,))],
+        compiler_params=pltpu.CompilerParams(vmem_limit_bytes=1024 * 1024),
     )(*results))
 
 

time: 24.4 us -> 21.9 us (0.90)
  local copies, waits for them, and re-layouts: 2.53 us -> 0 us
    unnamed x8 -> x0, local copies, waits for them, and re-layouts: 2.53 us -> none
    pallas_call x1, Pallas kernels: 1.81 us -> 0.78 us  [paired(): pl.pallas_call(leave, out_shape=outs, in_specs=[vmem] * 4, out_specs=[hbm...]
    pallas_call x1, Pallas kernels: 19.3 us -> 20.3 us  [paired(): pl.pallas_call(functools.partial(kernel, shards, heads), out_shape=[pltpu...]
where the time goes in v4:
time: 21.9 us; the launch traced here: 21.7 us
  Pallas kernels  21.1 us (96%)
  between operations  0.64 us (3%)
    pallas_call x1, Pallas kernels, paired(): pl.pallas_call(functools.partial(kernel, shards, heads), out_shape=[pltpu...  20.3 us
    pallas_call x1, Pallas kernels, paired(): pl.pallas_call(leave, out_shape=outs, in_specs=[vmem] * 4, out_specs=[hbm...  0.78 us

profile of v4, /device:TPU:5, one launch (start us, length us, event | category | flops | bytes accessed | tf_op | source)
XLA Modules:
  0.0 21.7 jit_solution(18271955375376593153)
XLA Ops:
  0.6 20.3 %shard_map.93 = (bf16[128,512]{1,0:T(8,128)(2,1)S(1)}, bf16[128,256]{1,0:T(8,128)(2,1)S(1)}, bf16[128,256]{1,0:T(8,128)(2,1)S(1)}, bf16[128,512]{1,0:T(8,128)(2,1)S(1)}) custom-call(bf16[32,1024]{1,0:T(8,128)(2,1)} %q_ref.1, bf16[32,1024]{1,0:T(8,128)(2,1)} %k_ref.1, bf16[32,2048]{1,0:T(8,128)(2,1)} %v_ref.1, bf16[128,512]{1,0:T(8,128)(2,1)} %g_ref.1, ...), custom_call_target="tpu_custom_call" | custom-call | tf_op jit(solution)/shard_map/pallas_call | solution.py:461
  21.0 0.8 %shard_map.94 = (bf16[128,512]{1,0:T(8,128)(2,1)}, bf16[128,256]{1,0:T(8,128)(2,1)}, bf16[128,256]{1,0:T(8,128)(2,1)}, bf16[128,512]{1,0:T(8,128)(2,1)}) custom-call(bf16[128,512]{1,0:T(8,128)(2,1)S(1)} %get-tuple-element.8.refs_0_, bf16[128,256]{1,0:T(8,128)(2,1)S(1)} %get-tuple-element.9.refs_1_, bf16[128,256]{1,0:T(8,128)(2,1)S(1)} %get-tuple-element.10.refs_2_, ...), custom_call_target="tpu_custom_call" | custom-call | tf_op jit(solution)/shard_map/pallas_call | solution.py:482

commit v5 on v3

--- a/solution.py
+++ b/solution.py
@@ -161,6 +161,7 @@
 
 CHUNKS = 4
 PARTS = 2
+HEADS = 4
 MESH = pl.DeviceIdType.MESH
 F32, BF16 = jnp.float32, jnp.bfloat16
 
@@ -213,19 +214,16 @@
     def _():
         pl.semaphore_signal(barrier, inc=1, device_id=(c + 1, h), device_id_type=MESH)
 
+    partners = (HEADS - 1 - h, lax.rem(h + 2, HEADS), h + 1 - 2 * lax.rem(h, 2))
+
     def head_copy(number, target_head, place_head):
-        if number < 2:
-            source, gathered = ((q_ref, q_all), (k_ref, k_all))[number]
-            span, place = key_dim, pl.ds(0, key_dim)
-            begin = target_head * key_dim
-        else:
-            source, gathered, span = v_ref, v_all, part
-            place = pl.ds((number - 2) * part, part)
-            begin = target_head * value_dim + (number - 2) * part
+        source, gathered = ((q_ref, q_all), (k_ref, k_all), (v_ref, v_all))[number]
+        span = gathered.shape[1]
+        begin = target_head * span
         held = pl.ds(pl.multiple_of(place_head * rows, rows), rows)
-        return source.at[:, pl.ds(pl.multiple_of(begin, span), span)], gathered.at[held, place]
-
-    pieces = 2 + PARTS
+        return source.at[:, pl.ds(pl.multiple_of(begin, span), span)], gathered.at[held]
+
+    pieces = 3
     own = [
         pltpu.make_async_copy(*head_copy(number, h, h), local_sem.at[number])
         for number in range(pieces)
@@ -242,22 +240,23 @@
         barrier, heads - 1 + has_earlier.astype(jnp.int32) + has_later.astype(jnp.int32)
     )
 
-    def exchanged(number, offset, incoming):
-        peer = lax.rem(h + (heads - offset if incoming else offset), heads)
+    def exchanged(number, p, incoming):
+        peer = partners[p]
         source, target = head_copy(number, peer, peer if incoming else h)
         return pltpu.make_async_remote_copy(
             src_ref=source, dst_ref=target,
-            send_sem=head_send.at[number, offset - 1], recv_sem=head_recv.at[number, offset - 1],
+            send_sem=head_send.at[number, p], recv_sem=head_recv.at[number, p],
             device_id=(c, peer), device_id_type=MESH,
         )
 
-    for offset in range(1, heads):
-        exchanged(0, offset, False).start()
+    for number in range(pieces):
+        for p in range(len(partners)):
+            exchanged(number, p, False).start()
 
     def arrived(number):
         own[number].wait()
-        for offset in range(1, heads):
-            exchanged(number, offset, True).wait_recv()
+        for p in range(len(partners)):
+            exchanged(number, p, True).wait_recv()
 
     for copy in small:
         copy.wait()
@@ -285,10 +284,6 @@
     tail = jnp.where(doc_col == doc_last, jnp.exp(cum_last - cum_col), 0.0)
     decay = jnp.where(doc_last == doc_before, jnp.exp(cum_last), 0.0)
 
-    for number in range(1, pieces):
-        for offset in range(1, heads):
-            exchanged(number, offset, False).start()
-
     def passing(update, first_out, first_in, state_out, state_in,
                 first_send, first_recv, state_send, state_recv, opens, target, has_source, has_target):
         closes = jnp.logical_not(opens)
@@ -352,68 +347,86 @@
                 for n in range(CHUNKS):
                     state_copy(n).wait_send()
 
-        return open_pair, close_pair, close_chunk, relay, finish
-
-    f_open, _, f_close_chunk, f_relay, f_finish = passing(
+        return open_pair, close_pair, relay, finish
+
+    f_open, f_close, f_relay, f_finish = passing(
         u_buf, f_first_out, f_first_in, f_state_out, f_state_in,
         f_first_send, f_first_recv, f_state_send, f_state_recv,
         even, c + 1, has_earlier, has_later,
     )
-    b_open, b_close, _, b_relay, b_finish = passing(
+    b_open, b_close, b_relay, b_finish = passing(
         w_buf, b_first_out, b_first_in, b_state_out, b_state_in,
         b_first_send, b_first_recv, b_state_send, b_state_recv,
         odd, c - 1, has_later, has_earlier,
     )
 
+    per_part = CHUNKS // PARTS
+
+    def halves(n):
+        return slice(n * part, (n + 1) * part)
+
     own_g.wait()
     arrived(0)
     queried = (q_all[...].astype(F32) * rate).T.astype(BF16)
+    product = dot(queried, g_all[...], 1, 0)
     for n in range(CHUNKS):
-        w_buf[n] = dot(queried, g_all[:, columns(n)], 1, 0)
+        w_buf[n] = product[:, columns(n)]
         b_open(n)
-    b_close()
 
     arrived(1)
     keyed = (k_all[...].astype(F32) * tail).T.astype(BF16)
+    arrived(2)
+    product = dot(keyed, v_all[...], 1, 0)
+    for n in range(CHUNKS):
+        u_buf[n] = product[:, columns(n)]
+        f_open(n)
+    b_close()
+    f_close()
+
     probs = (dot(q_all[...], k_all[...], 1, 1) * weights).astype(BF16)
+    gprobs = (dot(g_all[...], v_all[...], 1, 1) * weights).astype(BF16)
     dv_part[...] = dot(probs, g_all[...], 0, 0)
-    for n in range(CHUNKS):
-        if n % (CHUNKS // PARTS) == 0:
-            arrived(2 + n // (CHUNKS // PARTS))
-        u_buf[n] = dot(keyed, v_all[:, columns(n)], 1, 0)
-        f_open(n)
-        if n:
-            pl.when(odd)(functools.partial(f_close_chunk, n - 1))
-    pl.when(odd)(functools.partial(f_close_chunk, CHUNKS - 1))
-
-    gprobs = (dot(g_all[...], v_all[...], 1, 1) * weights).astype(BF16)
+    ret_part[...] = dot(probs, v_all[...], 1, 0)
     dk_part[...] = dot(gprobs, q_all[...], 0, 0)
     dq_part[...] = dot(gprobs, k_all[...], 1, 0)
-    ret_part[...] = dot(probs, v_all[...], 1, 0)
-
-    total = jnp.zeros((tokens, key_dim), F32)
-    for n in range(CHUNKS):
-        b_relay(n)
-        back = b_state_in[n]
-        dv_ref[:, columns(n)] = (
-            dot(k_all[...], back, 1, 0) * tail + dv_part[:, columns(n)]
-        ).astype(BF16)
-        total += dot(v_all[:, columns(n)], back, 1, 1)
-    dk_ref[...] = (total * tail + dk_part[...]).astype(BF16)
-
-    total = jnp.zeros((tokens, key_dim), F32)
-    for n in range(CHUNKS):
-        f_relay(n)
-        state = f_state_in[n]
-        ret_ref[:, columns(n)] = (
-            dot(q_all[...], state, 1, 0) * rate + ret_part[:, columns(n)]
-        ).astype(BF16)
-        total += dot(g_all[:, columns(n)], state, 1, 1)
-    dq_ref[...] = (total * rate + dq_part[...]).astype(BF16)
+
+    def directed(relay, state_in, left, right, factor, wide_part, narrow_part, wide_ref, narrow_ref, ahead):
+        if ahead:
+            for n in range(CHUNKS):
+                relay(n)
+        total = jnp.zeros((tokens, key_dim), F32)
+        for m in range(PARTS):
+            chunks = range(m * per_part, (m + 1) * per_part)
+            if not ahead:
+                for n in chunks:
+                    relay(n)
+            state = jnp.concatenate([state_in[n] for n in chunks], axis=1)
+            wide_ref[:, halves(m)] = (
+                dot(left[...], state, 1, 0) * factor + wide_part[:, halves(m)]
+            ).astype(BF16)
+            total += dot(right[:, halves(m)], state, 1, 1)
+        narrow_ref[...] = (total * factor + narrow_part[...]).astype(BF16)
+
+    forward = functools.partial(
+        directed, f_relay, f_state_in, q_all, g_all, rate, ret_part, dq_part, ret_ref, dq_ref
+    )
+    backward = functools.partial(
+        directed, b_relay, b_state_in, k_all, v_all, tail, dv_part, dk_part, dv_ref, dk_ref
+    )
+
+    @pl.when(even)
+    def _():
+        forward(True)
+        backward(False)
+
+    @pl.when(odd)
+    def _():
+        backward(True)
+        forward(False)
 
     for number in range(pieces):
-        for offset in range(1, heads):
-            exchanged(number, offset, False).wait_send()
+        for p in range(len(partners)):
+            exchanged(number, p, False).wait_send()
     b_finish()
     f_finish()
 
@@ -453,7 +466,7 @@
         + [total] * 2
         + [state] * 8
         + [pltpu.VMEM((tokens, width), F32) for width in wides]
-        + [dma((2 + PARTS, heads - 1)), dma((2 + PARTS, heads - 1)), dma((5 + PARTS,))]
+        + [dma((3, heads - 1)), dma((3, heads - 1)), dma((6,))]
         + [dma((CHUNKS,))] * 8,
         compiler_params=pltpu.CompilerParams(
             collective_id=0, has_side_effects=True, vmem_limit_bytes=40 * 1024 * 1024
@@ -468,6 +481,7 @@
         in_specs=[vmem] * 4,
         out_specs=[hbm] * 4,
         scratch_shapes=[dma((4,))],
+        compiler_params=pltpu.CompilerParams(vmem_limit_bytes=1024 * 1024),
     )(*results))
 
 
@@ -479,6 +493,7 @@
         tokens = window // shards
         reach = -(-(window // 4 - 1) // tokens)
         short = reach <= 2 and shards % 2 == 0 and tokens == BLOCK and (tokens // heads) % 16 == 0
+        short = short and heads == HEADS
         placed = (
             P(("ctx", "head"), None),
             P(("ctx", "head"), None),

time: 24.4 us -> 24 us (0.984); the launches traced: 24.3 us -> 23.6 us
  local copies, waits for them, and re-layouts: 2.53 us -> 0 us
  Pallas kernels: 21.1 us -> 23 us
    pallas_call x1, Pallas kernels: 19.3 us -> 22.2 us  [paired(): pl.pallas_call(functools.partial(kernel, shards, heads), out_shape=[pltpu...]
    unnamed x8 -> x0, local copies, waits for them, and re-layouts: 2.53 us -> none
    pallas_call x1, Pallas kernels: 1.81 us -> 0.78 us  [paired(): pl.pallas_call(leave, out_shape=outs, in_specs=[vmem] * 4, out_specs=[hbm...]
where the time goes in v5:
time: 24 us; the launch traced here: 23.6 us
  Pallas kernels  23 us (96%)
  between operations  0.64 us (3%)
    pallas_call x1, Pallas kernels, paired(): pl.pallas_call(functools.partial(kernel, shards, heads), out_shape=[pltpu...  22.2 us
    pallas_call x1, Pallas kernels, paired(): pl.pallas_call(leave, out_shape=outs, in_specs=[vmem] * 4, out_specs=[hbm...  0.78 us

profile of v5, /device:TPU:5, one launch (start us, length us, event | category | flops | bytes accessed | tf_op | source)
XLA Modules:
  0.0 23.6 jit_solution(5558153572829765016)
XLA Ops:
  0.6 22.2 %shard_map.93 = (bf16[128,512]{1,0:T(8,128)(2,1)S(1)}, bf16[128,256]{1,0:T(8,128)(2,1)S(1)}, bf16[128,256]{1,0:T(8,128)(2,1)S(1)}, bf16[128,512]{1,0:T(8,128)(2,1)S(1)}) custom-call(bf16[32,1024]{1,0:T(8,128)(2,1)} %q_ref.1, bf16[32,1024]{1,0:T(8,128)(2,1)} %k_ref.1, bf16[32,2048]{1,0:T(8,128)(2,1)} %v_ref.1, bf16[128,512]{1,0:T(8,128)(2,1)} %g_ref.1, ...), custom_call_target="tpu_custom_call" | custom-call | tf_op jit(solution)/shard_map/pallas_call | solution.py:457
  22.8 0.8 %shard_map.94 = (bf16[128,512]{1,0:T(8,128)(2,1)}, bf16[128,256]{1,0:T(8,128)(2,1)}, bf16[128,256]{1,0:T(8,128)(2,1)}, bf16[128,512]{1,0:T(8,128)(2,1)}) custom-call(bf16[128,512]{1,0:T(8,128)(2,1)S(1)} %get-tuple-element.8.refs_0_, bf16[128,256]{1,0:T(8,128)(2,1)S(1)} %get-tuple-element.9.refs_1_, bf16[128,256]{1,0:T(8,128)(2,1)S(1)} %get-tuple-element.10.refs_2_, ...), custom_call_target="tpu_custom_call" | custom-call | tf_op jit(solution)/shard_map/pallas_call | solution.py:478

commit v6 on v4

--- a/solution.py
+++ b/solution.py
@@ -251,8 +251,9 @@
             device_id=(c, peer), device_id_type=MESH,
         )
 
-    for offset in range(1, heads):
-        exchanged(0, offset, False).start()
+    for number in range(pieces):
+        for offset in range(1, heads):
+            exchanged(number, offset, False).start()
 
     def arrived(number):
         own[number].wait()
@@ -285,10 +286,6 @@
     tail = jnp.where(doc_col == doc_last, jnp.exp(cum_last - cum_col), 0.0)
     decay = jnp.where(doc_last == doc_before, jnp.exp(cum_last), 0.0)
 
-    for number in range(1, pieces - 1):
-        for offset in range(1, heads):
-            exchanged(number, offset, False).start()
-
     def passing(update, first_out, first_in, state_out, state_in,
                 first_send, first_recv, state_send, state_recv, opens, target, has_source, has_target):
         closes = jnp.logical_not(opens)
@@ -378,21 +375,18 @@
         for n in range(per_part):
             w_buf[m * per_part + n] = product[:, columns(n)]
             b_open(m * per_part + n)
-    for offset in range(1, heads):
-        exchanged(pieces - 1, offset, False).start()
     b_close()
 
     arrived(1)
     keyed = (k_all[...].astype(F32) * tail).T.astype(BF16)
     probs = (dot(q_all[...], k_all[...], 1, 1) * weights).astype(BF16)
+    dv_part[...] = dot(probs, g_all[...], 0, 0)
     for m in range(PARTS):
         arrived(2 + m)
         product = dot(keyed, v_all[:, halves(m)], 1, 0)
         for n in range(per_part):
             u_buf[m * per_part + n] = product[:, columns(n)]
             f_open(m * per_part + n)
-        if m == 0:
-            dv_part[...] = dot(probs, g_all[...], 0, 0)
 
         @pl.when(odd)
         def _():
@@ -404,29 +398,33 @@
     dq_part[...] = dot(gprobs, k_all[...], 1, 0)
     ret_part[...] = dot(probs, v_all[...], 1, 0)
 
-    def joined(relay, state_in, m):
-        chunks = range(m * per_part, (m + 1) * per_part)
-        for n in chunks:
-            relay(n)
-        return jnp.concatenate([state_in[n] for n in chunks], axis=1)
-
-    total = jnp.zeros((tokens, key_dim), F32)
-    for m in range(PARTS):
-        back = joined(b_relay, b_state_in, m)
-        dv_ref[:, halves(m)] = (
-            dot(k_all[...], back, 1, 0) * tail + dv_part[:, halves(m)]
-        ).astype(BF16)
-        total += dot(v_all[:, halves(m)], back, 1, 1)
-    dk_ref[...] = (total * tail + dk_part[...]).astype(BF16)
-
-    total = jnp.zeros((tokens, key_dim), F32)
-    for m in range(PARTS):
-        state = joined(f_relay, f_state_in, m)
-        ret_ref[:, halves(m)] = (
-            dot(q_all[...], state, 1, 0) * rate + ret_part[:, halves(m)]
-        ).astype(BF16)
-        total += dot(g_all[:, halves(m)], state, 1, 1)
-    dq_ref[...] = (total * rate + dq_part[...]).astype(BF16)
+    def directed(relay, state_in, left, right, factor, wide_part, narrow_part, wide_ref, narrow_ref, ahead):
+        if ahead:
+            for n in range(CHUNKS):
+                relay(n)
+        total = jnp.zeros((tokens, key_dim), F32)
+        for m in range(PARTS):
+            chunks = range(m * per_part, (m + 1) * per_part)
+            if not ahead:
+                for n in chunks:
+                    relay(n)
+            state = jnp.concatenate([state_in[n] for n in chunks], axis=1)
+            wide_ref[:, halves(m)] = (
+                dot(left[...], state, 1, 0) * factor + wide_part[:, halves(m)]
+            ).astype(BF16)
+            total += dot(right[:, halves(m)], state, 1, 1)
+        narrow_ref[...] = (total * factor + narrow_part[...]).astype(BF16)
+
+    forward = functools.partial(
+        directed, f_relay, f_state_in, q_all, g_all, rate, ret_part, dq_part, ret_ref, dq_ref
+    )
+    backward = functools.partial(
+        directed, b_relay, b_state_in, k_all, v_all, tail, dv_part, dk_part, dv_ref, dk_ref
+    )
+
+    backward(True)
+    pl.when(even)(lambda: forward(True))
+    pl.when(odd)(lambda: forward(False))
 
     for number in range(pieces):
         for offset in range(1, heads):

time: 21.9 us -> 20.9 us (0.954)
  Pallas kernels: 21.1 us -> 20.1 us
    pallas_call x1, Pallas kernels: 20.3 us -> 19.3 us  [paired(): pl.pallas_call(functools.partial(kernel, shards, heads), out_shape=[pltpu...]
where the time goes in v6:
time: 20.9 us; the launch traced here: 20.8 us
  Pallas kernels  20.1 us (96%)
  between operations  0.64 us (3%)
    pallas_call x1, Pallas kernels, paired(): pl.pallas_call(functools.partial(kernel, shards, heads), out_shape=[pltpu...  19.3 us
    pallas_call x1, Pallas kernels, paired(): pl.pallas_call(leave, out_shape=outs, in_specs=[vmem] * 4, out_specs=[hbm...  0.78 us

profile of v6, /device:TPU:5, one launch (start us, length us, event | category | flops | bytes accessed | tf_op | source)
XLA Modules:
  0.0 20.8 jit_solution(7028221674161293290)
XLA Ops:
  0.6 19.3 %shard_map.93 = (bf16[128,512]{1,0:T(8,128)(2,1)S(1)}, bf16[128,256]{1,0:T(8,128)(2,1)S(1)}, bf16[128,256]{1,0:T(8,128)(2,1)S(1)}, bf16[128,512]{1,0:T(8,128)(2,1)S(1)}) custom-call(bf16[32,1024]{1,0:T(8,128)(2,1)} %q_ref.1, bf16[32,1024]{1,0:T(8,128)(2,1)} %k_ref.1, bf16[32,2048]{1,0:T(8,128)(2,1)} %v_ref.1, bf16[128,512]{1,0:T(8,128)(2,1)} %g_ref.1, ...), custom_call_target="tpu_custom_call" | custom-call | tf_op jit(solution)/shard_map/pallas_call | solution.py:459
  20.0 0.8 %shard_map.94 = (bf16[128,512]{1,0:T(8,128)(2,1)}, bf16[128,256]{1,0:T(8,128)(2,1)}, bf16[128,256]{1,0:T(8,128)(2,1)}, bf16[128,512]{1,0:T(8,128)(2,1)}) custom-call(bf16[128,512]{1,0:T(8,128)(2,1)S(1)} %get-tuple-element.8.refs_0_, bf16[128,256]{1,0:T(8,128)(2,1)S(1)} %get-tuple-element.9.refs_1_, bf16[128,256]{1,0:T(8,128)(2,1)S(1)} %get-tuple-element.10.refs_2_, ...), custom_call_target="tpu_custom_call" | custom-call | tf_op jit(solution)/shard_map/pallas_call | solution.py:480

commit v7 on v6

--- a/solution.py
+++ b/solution.py
@@ -393,6 +393,11 @@
             for n in range(per_part):
                 f_close_chunk(m * per_part + n)
 
+    @pl.when(odd)
+    def _():
+        for n in range(CHUNKS):
+            b_relay(n)
+
     gprobs = (dot(g_all[...], v_all[...], 1, 1) * weights).astype(BF16)
     dk_part[...] = dot(gprobs, q_all[...], 0, 0)
     dq_part[...] = dot(gprobs, k_all[...], 1, 0)
@@ -405,7 +410,7 @@
         total = jnp.zeros((tokens, key_dim), F32)
         for m in range(PARTS):
             chunks = range(m * per_part, (m + 1) * per_part)
-            if not ahead:
+            if ahead is False:
                 for n in chunks:
                     relay(n)
             state = jnp.concatenate([state_in[n] for n in chunks], axis=1)
@@ -422,9 +427,15 @@
         directed, b_relay, b_state_in, k_all, v_all, tail, dv_part, dk_part, dv_ref, dk_ref
     )
 
-    backward(True)
-    pl.when(even)(lambda: forward(True))
-    pl.when(odd)(lambda: forward(False))
+    @pl.when(even)
+    def _():
+        backward(False)
+        forward(True)
+
+    @pl.when(odd)
+    def _():
+        backward(None)
+        forward(False)
 
     for number in range(pieces):
         for offset in range(1, heads):

time: 20.9 us -> 21 us (level)
  no operation moved by 1% of the time
where the time goes in v7:
time: 21 us; the launch traced here: 20.8 us
  Pallas kernels  20.2 us (96%)
  between operations  0.64 us (3%)
    pallas_call x1, Pallas kernels, paired(): pl.pallas_call(functools.partial(kernel, shards, heads), out_shape=[pltpu...  19.4 us
    pallas_call x1, Pallas kernels, paired(): pl.pallas_call(leave, out_shape=outs, in_specs=[vmem] * 4, out_specs=[hbm...  0.78 us

profile of v7, /device:TPU:5, one launch (start us, length us, event | category | flops | bytes accessed | tf_op | source)
XLA Modules:
  0.0 20.8 jit_solution(16743466627051668746)
XLA Ops:
  0.6 19.4 %shard_map.93 = (bf16[128,512]{1,0:T(8,128)(2,1)S(1)}, bf16[128,256]{1,0:T(8,128)(2,1)S(1)}, bf16[128,256]{1,0:T(8,128)(2,1)S(1)}, bf16[128,512]{1,0:T(8,128)(2,1)S(1)}) custom-call(bf16[32,1024]{1,0:T(8,128)(2,1)} %q_ref.1, bf16[32,1024]{1,0:T(8,128)(2,1)} %k_ref.1, bf16[32,2048]{1,0:T(8,128)(2,1)} %v_ref.1, bf16[128,512]{1,0:T(8,128)(2,1)} %g_ref.1, ...), custom_call_target="tpu_custom_call" | custom-call | tf_op jit(solution)/shard_map/pallas_call | solution.py:470
  20.1 0.8 %shard_map.94 = (bf16[128,512]{1,0:T(8,128)(2,1)}, bf16[128,256]{1,0:T(8,128)(2,1)}, bf16[128,256]{1,0:T(8,128)(2,1)}, bf16[128,512]{1,0:T(8,128)(2,1)}) custom-call(bf16[128,512]{1,0:T(8,128)(2,1)S(1)} %get-tuple-element.8.refs_0_, bf16[128,256]{1,0:T(8,128)(2,1)S(1)} %get-tuple-element.9.refs_1_, bf16[128,256]{1,0:T(8,128)(2,1)S(1)} %get-tuple-element.10.refs_2_, ...), custom_call_target="tpu_custom_call" | custom-call | tf_op jit(solution)/shard_map/pallas_call | solution.py:491
